TPU v7x, 128 devices: a whole 4x4x4 slice. The times are simulated.
128 devices in a mesh: seq: 16 (over z, y), dp: 8 (over x, core).
Axes of the slice: x: 4, y: 4, z: 4, core: 2. Of those that a mesh axis runs over, the one named last changes fastest.
Arguments:
- reader_rows: float32 [8, 2048, 6144], P('dp', 'seq'), may hold values from -40 to 40
- reader_targets: float32 [8, 2048, 2048], P('dp', 'seq'), may hold values from -3 to 3
- dest_pos: int32 [8, 2048], P('dp', 'seq'), may hold values from 0 to 2047, as said below
- bucket_ids: int32 [8, 2048], P('dp', 'seq'), may hold values from 0 to 15, as said below
- ref_loss: float32 [8, 2048], P('dp', 'seq'), may hold values from 0.1 to 0.6
- timesteps: int32 [8], P('dp'), may hold values from 0 to 999
- mod_weight: float32 [256, 2048], replicated, may hold values from -0.75 to 0.75
- mixture_old: float32 [16], replicated, may hold values from 0.25 to 4
Outputs:
- attended: float32 [8, 2048, 2048], P('dp', 'seq')
- qkv_grad: float32 [8, 2048, 6144], P('dp', 'seq')
- mod_weight_grad: float32 [256, 2048], replicated
- mixture: float32 [16], replicated
Inputs may be any that keep to these rules, and one draw needn't show every extreme that they name: `dest_pos`: the positions of one sample form a permutation of the sequence; the rows of one device go at most 16 to any one sequence shard (positions k * 128 to (k + 1) * 128 - 1), and every device sends exactly 16 rows to some shard. `bucket_ids`: A bucket may hold no position at all.
All inputs are finite; a program needn't handle non-finite values.
Results may differ from a plain program's by a relative error of at most 0.0003.
Values sent between devices are 32-bit elements; how exact they have to be, the bound alone decides.
A program may use at most 128 MiB of HBM per device.

v0:
```python
import math

import jax
import jax.numpy as jnp
from jax import lax
from jax.sharding import PartitionSpec as P

HEADS = 16
HEAD_DIM = 128
FREQ_DIM = 256
BUCKETS = 16


highest = lax.Precision.HIGHEST
excess_rate = 10.0


def embed_time(timesteps):
    half_dim = FREQ_DIM // 2
    frequency = jnp.exp(-math.log(10000.0) * jnp.arange(half_dim, dtype=jnp.float32) / half_dim)
    angles = timesteps.astype(jnp.float32)[:, None] * frequency[None, :]
    return jax.nn.silu(jnp.concatenate([jnp.cos(angles), jnp.sin(angles)], axis=1))


def pack_slots(values_list, positions, local_rows, shards, slot_count):
    owner_shard = positions // local_rows
    match = (owner_shard[:, None] == jnp.arange(shards)[None, :]).astype(jnp.int32)
    before = jnp.cumsum(match, axis=0) - match
    within = jnp.sum(before * match, axis=1)
    target_slot = owner_shard * slot_count + within
    packed = tuple(
        (
            jnp.zeros((shards * slot_count,) + item.shape[1:], item.dtype)
            .at[target_slot]
            .set(item)
            .reshape((shards, slot_count) + item.shape[1:])
            for item in values_list
        )
    )
    tag_list = (
        jnp.full((shards * slot_count,), -1, jnp.int32)
        .at[target_slot]
        .set(positions)
        .reshape(shards, slot_count)
    )
    return (packed, tag_list)


def unpack_slots(received, tag_list, my_index, local_rows):
    flat_tags = tag_list.reshape(-1)
    place_at = jnp.where(flat_tags >= 0, flat_tags - my_index * local_rows, local_rows)
    return tuple(
        (
            jnp.zeros((local_rows,) + item.shape[2:], item.dtype)
            .at[place_at]
            .set(item.reshape((-1,) + item.shape[2:]), mode="drop")
            for item in received
        )
    )


def block_probs(query_rows, key_all, softmax_scale):
    scores = jnp.einsum("qhd,khd->hqk", query_rows, key_all, precision=highest) * softmax_scale
    row_top = jnp.max(scores, axis=2, keepdims=True)
    expweights = jnp.exp(scores - row_top)
    return expweights / jnp.sum(expweights, axis=2, keepdims=True)


def attend_forward(query_all, key_all, value_all, block):
    softmax_scale = HEAD_DIM ** (-0.5)
    block_count = query_all.shape[0] // block
    query_blocks = query_all.reshape(block_count, block, query_all.shape[1], HEAD_DIM)

    def one_block(query_rows):
        probability = block_probs(query_rows, key_all, softmax_scale)
        return jnp.einsum("hqk,khd->qhd", probability, value_all, precision=highest)

    return lax.map(one_block, query_blocks).reshape(query_all.shape)


def attend_backward(query_all, key_all, value_all, output_all, upstream_all, block):
    softmax_scale = HEAD_DIM ** (-0.5)
    block_count = query_all.shape[0] // block
    split_shape = (block_count, block, query_all.shape[1], HEAD_DIM)

    def block_step(running, packed):
        key_grad, value_grad = running
        query_rows, output_rows, upstream_rows = packed
        probability = block_probs(query_rows, key_all, softmax_scale)
        prob_grad = jnp.einsum("qhd,khd->hqk", upstream_rows, value_all, precision=highest)
        row_delta = jnp.sum(upstream_rows * output_rows, axis=2).T[:, :, None]
        score_grad = probability * (prob_grad - row_delta)
        query_grad = softmax_scale * jnp.einsum(
            "hqk,khd->qhd", score_grad, key_all, precision=highest
        )
        key_grad = key_grad + softmax_scale * jnp.einsum(
            "hqk,qhd->khd", score_grad, query_rows, precision=highest
        )
        value_grad = value_grad + jnp.einsum(
            "hqk,qhd->khd", probability, upstream_rows, precision=highest
        )
        return ((key_grad, value_grad), query_grad)

    start_grads = (jnp.zeros_like(key_all), jnp.zeros_like(value_all))
    (key_grad, value_grad), query_grad = lax.scan(
        block_step,
        start_grads,
        (
            query_all.reshape(split_shape),
            output_all.reshape(split_shape),
            upstream_all.reshape(split_shape),
        ),
    )
    return (query_grad.reshape(query_all.shape), key_grad, value_grad)


def body(
    reader_rows, reader_targets, dest_pos, bucket_ids, ref_loss, timesteps, mod_weight, mixture_old
):
    shards = lax.axis_size("seq")
    my_index = lax.axis_index("seq")
    local_rows = reader_rows.shape[1]
    full_length = local_rows * shards
    head_count = HEADS // shards
    channel_count = head_count * HEAD_DIM
    slot_count = 2 * local_rows // shards
    block = math.gcd(512, full_length)
    row_data = reader_rows[0]
    aim_data = reader_targets[0]
    positions = dest_pos[0]
    onehot = (bucket_ids[0][:, None] == jnp.arange(BUCKETS)[None, :]).astype(jnp.float32)
    row_weight = jnp.sum(onehot * mixture_old[None, :], axis=1)
    packed, tag_list = pack_slots((row_data, aim_data), positions, local_rows, shards, slot_count)
    received = (
        lax.all_to_all(packed[0], "seq", split_axis=0, concat_axis=0, tiled=True),
        lax.all_to_all(packed[1], "seq", split_axis=0, concat_axis=0, tiled=True),
    )
    got_tags = lax.all_to_all(tag_list, "seq", split_axis=0, concat_axis=0, tiled=True)
    seq_rows, seq_aims = unpack_slots(received, got_tags, my_index, local_rows)
    head_data, head_aims = (
        lax.all_to_all(
            seq_rows.reshape(local_rows, 3, HEADS, HEAD_DIM),
            "seq",
            split_axis=2,
            concat_axis=0,
            tiled=True,
        ),
        lax.all_to_all(
            seq_aims.reshape(local_rows, 1, HEADS, HEAD_DIM),
            "seq",
            split_axis=2,
            concat_axis=0,
            tiled=True,
        ),
    )
    all_weights = lax.all_gather(row_weight, "seq", axis=0, tiled=True)
    query_all = head_data[:, 0]
    key_all = head_data[:, 1]
    value_all = head_data[:, 2]
    aims_all = head_aims[:, 0]
    output_all = attend_forward(query_all, key_all, value_all, block)
    embedding = embed_time(timesteps)
    modulation = 1.0 + jnp.dot(embedding, mod_weight, precision=highest)
    head_gain = lax.dynamic_slice_in_dim(
        modulation[0], my_index * channel_count, channel_count
    ).reshape(head_count, HEAD_DIM)
    attended_heads = head_gain[None] * output_all
    gap = attended_heads - aims_all
    partial_loss = jnp.sum(gap * gap, axis=(1, 2))
    upstream_a = all_weights[:, None, None] * gap
    upstream_heads = head_gain[None] * upstream_a
    gain_local = jnp.sum(upstream_a * output_all, axis=0).reshape(channel_count)
    gain_part = lax.dynamic_update_slice_in_dim(
        jnp.zeros((HEADS * HEAD_DIM,), jnp.float32), gain_local, my_index * channel_count, 0
    )
    seq_heads, loss_parts = (
        lax.all_to_all(attended_heads, "seq", split_axis=0, concat_axis=1, tiled=True),
        lax.all_to_all(partial_loss[:, None], "seq", split_axis=0, concat_axis=1, tiled=True),
    )
    attended = seq_heads.reshape(local_rows, HEADS * HEAD_DIM)
    row_loss = 0.5 * jnp.sum(loss_parts, axis=1) / (HEADS * HEAD_DIM)
    excess = jnp.maximum(row_loss - ref_loss[0], 0.0)
    bucket_sums, bucket_counts = lax.psum(
        (jnp.sum(onehot * excess[:, None], axis=0), jnp.sum(onehot, axis=0)), ("seq", "dp")
    )
    query_grad, key_grad, value_grad = attend_backward(
        query_all, key_all, value_all, output_all, upstream_heads, block
    )
    stacked = jnp.stack([query_grad, key_grad, value_grad], axis=1)
    seq_grads = lax.all_to_all(stacked, "seq", split_axis=0, concat_axis=2, tiled=True).reshape(
        local_rows, 3 * HEADS * HEAD_DIM
    )
    weight_grad = lax.psum(
        jnp.dot(embedding.T, gain_part[None, :], precision=highest), ("seq", "dp")
    )
    bucket_excess = bucket_sums / jnp.maximum(bucket_counts, 1.0)
    updated = mixture_old * (1.0 + excess_rate * bucket_excess)
    mixture = BUCKETS * updated / jnp.sum(updated)
    return (attended[None], seq_grads[None], weight_grad, mixture)


def solution(mesh):
    return jax.shard_map(
        body,
        mesh=mesh,
        in_specs=(
            P("dp", "seq", None),
            P("dp", "seq", None),
            P("dp", "seq"),
            P("dp", "seq"),
            P("dp", "seq"),
            P("dp"),
            P(),
            P(),
        ),
        out_specs=(P("dp", "seq", None), P("dp", "seq", None), P(), P()),
        check_vma=False,
    )
```

profile of v0, /device:TPU:1, one launch (start us, length us, event | category | flops | bytes accessed | tf_op | source)
XLA Modules:
  0.0 644.3 jit_solution(9777270074004782485)
XLA Ops:
  10.9 8.6 %all-to-all-start = ((s32[16,1,16]{2,1,0:T(1,128)}), s32[16,1,16]{2,1,0:T(1,128)S(1)}, u32[]{:S(2)}, u32[]{:S(2)}) async-start(s32[16,1,16]{2,1,0:T(1,128)} %all_to_all.68), calls=%async_computation | async-start | bytes 16384 | tf_op jit(solution)/shard_map/all_to_all | solution.py:138
  19.5 3.4 scatter_custom_fusion.3
  22.9 2.9 all-to-all-done
  25.9 4.4 all-to-all-start.4
  30.3 5.5 scatter_custom_fusion.1
  35.8 21.3 %all-to-all-done.4 = f32[16,16,2048]{2,1,0:T(8,128)} async-done(((f32[16,16,2048]{2,1,0:T(8,128)}), f32[16,16,2048]{2,1,0:T(8,128)}, u32[]{:S(2)}, u32[]{:S(2)}) %all-to-all-start.4) | async-done | bytes 2097184 | tf_op jit(solution)/shard_map/all_to_all | solution.py:136
  57.1 6.9 %all-to-all-start.1 = ((f32[16,16,6144]{2,1,0:T(8,128)}), f32[16,16,6144]{2,1,0:T(8,128)}, u32[]{:S(2)}, u32[]{:S(2)}) async-start(f32[16,16,6144]{2,1,0:T(8,128)} %bitcast.209), calls=%async_computation.1 | async-start | bytes 12582912 | tf_op jit(solution)/shard_map/all_to_all | solution.py:135
  64.1 3.1 scatter_custom_fusion.4
  68.6 85.1 %all-to-all-done.1 = f32[16,16,6144]{2,1,0:T(8,128)} async-done(((f32[16,16,6144]{2,1,0:T(8,128)}), f32[16,16,6144]{2,1,0:T(8,128)}, u32[]{:S(2)}, u32[]{:S(2)}) %all-to-all-start.1) | async-done | bytes 6291488 | tf_op jit(solution)/shard_map/all_to_all | solution.py:135
  153.6 5.0 all-to-all-start.5
  158.6 7.2 %scatter_custom_fusion.2 = f32[128,6144]{1,0:T(8,128)S(1)} fusion(s32[256]{0:T(256)S(1)} %bitcast.227, f32[256,6144]{1,0:T(8,128)} %bitcast.17, f32[]{:T(128)} %constant.97.clone.1), kind=kCustom, calls=%fused_computation.28 | custom fusion | bytes 3146240 | tf_op jit(solution)/shard_map/scatter | solution.py:56
  165.9 2.4 copy.64
  168.2 3.9 copy.65
  172.5 6.5 %all-to-all-start.2 = ((f32[128,3,16,128]{0,3,1,2:T(8,128)}), f32[128,3,16,128]{0,3,1,2:T(8,128)}, u32[]{:S(2)}, u32[]{:S(2)}) async-start(f32[128,3,16,128]{0,3,1,2:T(8,128)} %copy.65), calls=%async_computation.2 | async-start | bytes 6291456 | tf_op jit(solution)/shard_map/all_to_all | solution.py:141
  180.9 2.6 copy.73
  183.5 32.4 %all-to-all-done.2 = f32[128,3,16,128]{0,3,1,2:T(8,128)} async-done(((f32[128,3,16,128]{0,3,1,2:T(8,128)}), f32[128,3,16,128]{0,3,1,2:T(8,128)}, u32[]{:S(2)}, u32[]{:S(2)}) %all-to-all-start.2) | async-done | bytes 3145760 | tf_op jit(solution)/shard_map/all_to_all | solution.py:141
  215.9 3.5 copy.66
  219.4 3.5 fusion.33
  223.9 51.8 %while.25 = (s32[]{:T(128)}, f32[4,512,1,128]{3,1,2,0:T(8,128)}, f32[4,512,1,128]{3,2,1,0:T(1,128)}, f32[2048,1,128]{2,1,0:T(1,128)S(1)}, f32[2048,1,128]{2,0,1:T(8,128)S(1)}, /*index=5*/s32[]{:T(128)}) while((s32[]{:T(128)}, f32[4,512,1,128]{3,1,2,0:T(8,128)}, f32[4,512,1,128]{3,2,1,0:T(1,128)}, f32[2048,1,128]{2,1,0:T(1,128)S(1)}, ...), condition=%wide.region_8.9_spmd, body=%wide.region_5.8_spmd.sunk | while | flops 1611661312 | bytes 11534921 | solution.py:78
  224.9 5.0 convolution_multiply_fusion.4
  229.9 7.0 %online-softmax.1 = f32[4,512,1,128]{3,1,2,0:T(8,128)} fusion(f32[4,512,1,128]{3,1,2,0:T(8,128)} %get-tuple-element.347, s32[]{:T(128)} %get-tuple-element.346, f32[512,2048]{1,0:T(8,128)} %convolution_multiply_fusion.4, f32[2048,128]{1,0:T(8,128)S(1)} %bitcast.202), kind=kCustom, calls=%fused_computation.6.clone.1 | custom fusion | bytes 5505536 | tf_op online-softmax
  237.8 5.0 convolution_multiply_fusion.4
  242.8 7.0 %online-softmax.1 = f32[4,512,1,128]{3,1,2,0:T(8,128)} fusion(f32[4,512,1,128]{3,1,2,0:T(8,128)} %get-tuple-element.347, s32[]{:T(128)} %get-tuple-element.346, f32[512,2048]{1,0:T(8,128)} %convolution_multiply_fusion.4, f32[2048,128]{1,0:T(8,128)S(1)} %bitcast.202), kind=kCustom, calls=%fused_computation.6.clone.1 | custom fusion | bytes 5505536 | tf_op online-softmax
  250.8 5.0 convolution_multiply_fusion.4
  255.8 7.0 %online-softmax.1 = f32[4,512,1,128]{3,1,2,0:T(8,128)} fusion(f32[4,512,1,128]{3,1,2,0:T(8,128)} %get-tuple-element.347, s32[]{:T(128)} %get-tuple-element.346, f32[512,2048]{1,0:T(8,128)} %convolution_multiply_fusion.4, f32[2048,128]{1,0:T(8,128)S(1)} %bitcast.202), kind=kCustom, calls=%fused_computation.6.clone.1 | custom fusion | bytes 5505536 | tf_op online-softmax
  263.7 5.0 convolution_multiply_fusion.4
  268.7 7.0 %online-softmax.1 = f32[4,512,1,128]{3,1,2,0:T(8,128)} fusion(f32[4,512,1,128]{3,1,2,0:T(8,128)} %get-tuple-element.347, s32[]{:T(128)} %get-tuple-element.346, f32[512,2048]{1,0:T(8,128)} %convolution_multiply_fusion.4, f32[2048,128]{1,0:T(8,128)S(1)} %bitcast.202), kind=kCustom, calls=%fused_computation.6.clone.1 | custom fusion | bytes 5505536 | tf_op online-softmax
  275.7 2.6 fusion.14
  278.3 9.3 %all-to-all-start.7 = ((f32[16,128,1]{1,2,0:T(1,128)}), f32[16,128,1]{1,2,0:T(1,128)S(1)}, u32[]{:S(2)}, u32[]{:S(2)}) async-start(f32[16,128,1]{1,2,0:T(1,128)} %bitcast.57), calls=%async_computation.7 | async-start | bytes 16384 | tf_op jit(solution)/shard_map/all_to_all | solution.py:178
  287.6 2.6 broadcast_multiply_fusion.1
  290.2 3.7 all-to-all-done.7
  293.9 4.4 all-to-all-start.3
  298.5 24.5 %all-gather = f32[16,1,128]{2,1,0:T(1,128)S(1)} all-gather(f32[1,1,128]{2,1,0:T(1,128)S(1)} %bitcast.225), channel_id=1, replica_groups=mesh['seq'=16,'dp'=8] {'seq'}, dimensions={0}, use_global_device_ids=true | all-gather | bytes 8704 | tf_op jit(solution)/shard_map/all_gather | solution.py:156
  324.2 2.5 fusion.19
  327.9 119.3 %while.26 = (s32[]{:T(128)}, f32[2048,1,128]{0,2,1:T(8,128)S(1)}, f32[2048,1,128]{0,2,1:T(8,128)}, f32[4,512,1,128]{3,1,2,0:T(8,128)}, f32[4,512,1,128]{3,2,1,0:...) while((s32[]{:T(128)}, f32[2048,1,128]{0,2,1:T(8,128)S(1)}, ...), condition=%wide.region_16.17_spmd.clone, body=%wide.region_12.16_spmd.clone.sunk | while | flops 8068200960 | bytes 81283824 | solution.py:105
  340.8 2.2 multiply_reduce_fusion.4
  342.9 3.8 multiply_reduce_fusion.5
  349.5 6.5 %fusion.78 = f32[2048,1,128]{0,2,1:T(8,128)} fusion(f32[512,128]{1,0:T(8,128)S(1)} %bitcast.215, f32[2048,1,128]{0,2,1:T(8,128)} %get-tuple-element.371, pred[]{:T(512)S(6)} %compare.17, f32[512,2048]{1,0:T(8,128)} %copy-done.2, f32[512]{0:T(512)S(1)} %fusion.76, f32[512]{0:T(512)S(1)} %get-tuple-element.339), kind=kOutput, calls=%fused_computation.17.clone.1 | convolution fusion | flops 1614282752 | bytes 6557697 | tf_op jit(solution)/shard_map/while/body/eval_jaxpr/hqk,qhd->khd/dot_general | solution.py:99
  356.0 4.4 subtract_multiply_fusion.2
  360.4 2.6 fusion.77
  363.0 4.1 fusion.79
  367.1 2.2 multiply_reduce_fusion.4
  369.3 3.8 multiply_reduce_fusion.5
  375.8 6.8 %fusion.78 = f32[2048,1,128]{0,2,1:T(8,128)} fusion(f32[512,128]{1,0:T(8,128)S(1)} %bitcast.215, f32[2048,1,128]{0,2,1:T(8,128)} %get-tuple-element.371, pred[]{:T(512)S(6)} %compare.17, f32[512,2048]{1,0:T(8,128)} %copy-done.2, f32[512]{0:T(512)S(1)} %fusion.76, f32[512]{0:T(512)S(1)} %get-tuple-element.339), kind=kOutput, calls=%fused_computation.17.clone.1 | convolution fusion | flops 1614282752 | bytes 6557697 | tf_op jit(solution)/shard_map/while/body/eval_jaxpr/hqk,qhd->khd/dot_general | solution.py:99
  382.6 4.4 subtract_multiply_fusion.2
  387.0 2.6 fusion.77
  389.6 4.1 fusion.79
  395.9 3.8 multiply_reduce_fusion.5
  402.4 6.8 %fusion.78 = f32[2048,1,128]{0,2,1:T(8,128)} fusion(f32[512,128]{1,0:T(8,128)S(1)} %bitcast.215, f32[2048,1,128]{0,2,1:T(8,128)} %get-tuple-element.371, pred[]{:T(512)S(6)} %compare.17, f32[512,2048]{1,0:T(8,128)} %copy-done.2, f32[512]{0:T(512)S(1)} %fusion.76, f32[512]{0:T(512)S(1)} %get-tuple-element.339), kind=kOutput, calls=%fused_computation.17.clone.1 | convolution fusion | flops 1614282752 | bytes 6557697 | tf_op jit(solution)/shard_map/while/body/eval_jaxpr/hqk,qhd->khd/dot_general | solution.py:99
  409.2 4.4 subtract_multiply_fusion.2
  413.6 2.6 fusion.77
  416.2 4.2 fusion.79
  422.5 3.8 multiply_reduce_fusion.5
  429.1 6.8 %fusion.78 = f32[2048,1,128]{0,2,1:T(8,128)} fusion(f32[512,128]{1,0:T(8,128)S(1)} %bitcast.215, f32[2048,1,128]{0,2,1:T(8,128)} %get-tuple-element.371, pred[]{:T(512)S(6)} %compare.17, f32[512,2048]{1,0:T(8,128)} %copy-done.2, f32[512]{0:T(512)S(1)} %fusion.76, f32[512]{0:T(512)S(1)} %get-tuple-element.339), kind=kOutput, calls=%fused_computation.17.clone.1 | convolution fusion | flops 1614282752 | bytes 6557697 | tf_op jit(solution)/shard_map/while/body/eval_jaxpr/hqk,qhd->khd/dot_general | solution.py:99
  435.8 4.4 subtract_multiply_fusion.2
  440.2 2.6 fusion.77
  442.8 4.2 fusion.79
  449.1 6.0 pad_maximum_fusion
  455.1 4.5 all-to-all-start.6
  461.4 93.7 %all-reduce = (f32[16]{0:T(128)S(1)}, f32[16]{0:T(128)S(1)}) all-reduce(f32[16]{0:T(128)S(1)} %get-tuple-element.197, f32[16]{0:T(128)S(1)} %get-tuple-element.196), channel_id=1, replica_groups=mesh['seq'=16,'dp'=8] {'seq','dp'}, use_global_device_ids=true, to_apply=%region_22.23 | all-reduce | flops 32 | bytes 256 | tf_op jit(solution)/shard_map/psum | solution.py:183
  559.8 5.6 copy.81
  565.4 4.2 broadcast_in_dim_reshape.9
  569.6 64.3 %all-reduce.3.cloned.1.call-done = f32[256,2048]{1,0:T(8,128)} async-done(((f32[256,2048]{1,0:T(8,128)}), f32[256,2048]{1,0:T(8,128)}) %all-reduce.3.cloned.1.call-update) | async-done | bytes 2097168 | tf_op jit(solution)/shard_map/psum | solution.py:193
  633.9 3.1 copy.112
  (95 shorter events, 37.8 us)
Async XLA Ops:
  7.2 23.1 %copy-start = (f32[1,128,6144]{2,1,0:T(8,128)S(1)}, f32[1,128,6144]{2,1,0:T(8,128)}, u32[]{:S(2)}) copy-start(f32[1,128,6144]{2,1,0:T(8,128)} %param.12) | copy-start | bytes 9437188
  10.9 14.9 %all-to-all-start = ((s32[16,1,16]{2,1,0:T(1,128)}), s32[16,1,16]{2,1,0:T(1,128)S(1)}, u32[]{:S(2)}, u32[]{:S(2)}) async-start(s32[16,1,16]{2,1,0:T(1,128)} %all_to_all.68), calls=%async_computation | async-start | bytes 16384 | tf_op jit(solution)/shard_map/all_to_all | solution.py:138
  25.9 31.3 %all-to-all-start.4 = ((f32[16,16,2048]{2,1,0:T(8,128)}), f32[16,16,2048]{2,1,0:T(8,128)}, u32[]{:S(2)}, u32[]{:S(2)}) async-start(f32[16,16,2048]{2,1,0:T(8,128)} %bitcast.214), calls=%async_computation.4 | async-start | bytes 4194304 | tf_op jit(solution)/shard_map/all_to_all | solution.py:136
  57.1 96.5 %all-to-all-start.1 = ((f32[16,16,6144]{2,1,0:T(8,128)}), f32[16,16,6144]{2,1,0:T(8,128)}, u32[]{:S(2)}, u32[]{:S(2)}) async-start(f32[16,16,6144]{2,1,0:T(8,128)} %bitcast.209), calls=%async_computation.1 | async-start | bytes 12582912 | tf_op jit(solution)/shard_map/all_to_all | solution.py:135
  153.6 18.8 %all-to-all-start.5 = ((f32[128,1,16,128]{0,3,1,2:T(8,128)}), f32[128,1,16,128]{0,3,1,2:T(8,128)}, u32[]{:S(2)}, u32[]{:S(2)}) async-start(f32[128,1,16,128]{0,3,1,2:T(8,128)} %bitcast.42), calls=%async_computation.5 | async-start | bytes 2097152 | tf_op jit(solution)/shard_map/all_to_all | solution.py:148
  172.2 7.5 %copy-start.6 = (f32[256,2048]{1,0:T(8,128)S(1)}, f32[256,2048]{1,0:T(8,128)}, u32[]{:S(2)}) copy-start(f32[256,2048]{1,0:T(8,128)} %param.18) | copy-start | bytes 6291460
  172.5 43.4 %all-to-all-start.2 = ((f32[128,3,16,128]{0,3,1,2:T(8,128)}), f32[128,3,16,128]{0,3,1,2:T(8,128)}, u32[]{:S(2)}, u32[]{:S(2)}) async-start(f32[128,3,16,128]{0,3,1,2:T(8,128)} %copy.65), calls=%async_computation.2 | async-start | bytes 6291456 | tf_op jit(solution)/shard_map/all_to_all | solution.py:141
  275.7 22.6 %copy-start.10 = (f32[1,128]{1,0:T(1,128)S(1)}, f32[1,128]{1,0:T(1,128)}, u32[]{:S(2)}) copy-start(f32[1,128]{1,0:T(1,128)} %param.16) | copy-start | bytes 1540
  275.7 22.7 %copy-start.8 = (f32[16]{0:T(128)S(1)}, f32[16]{0:T(128)}, u32[]{:S(2)}) copy-start(f32[16]{0:T(128)} %param.19) | copy-start | bytes 196
  275.7 22.7 %copy-start.9 = (s32[1,128]{1,0:T(1,128)S(1)}, s32[1,128]{1,0:T(1,128)}, u32[]{:S(2)}) copy-start(s32[1,128]{1,0:T(1,128)} %param.15) | copy-start | bytes 1540
  275.7 48.5 %copy-start.4 = (f32[4,512,1,128]{3,1,2,0:T(8,128)S(1)}, f32[4,512,1,128]{3,1,2,0:T(8,128)}, u32[]{:S(2)}) copy-start(f32[4,512,1,128]{3,1,2,0:T(8,128)} %get-tuple-element.191) | copy-start | bytes 3145732
  278.3 15.7 %all-to-all-start.7 = ((f32[16,128,1]{1,2,0:T(1,128)}), f32[16,128,1]{1,2,0:T(1,128)S(1)}, u32[]{:S(2)}, u32[]{:S(2)}) async-start(f32[16,128,1]{1,2,0:T(1,128)} %bitcast.57), calls=%async_computation.7 | async-start | bytes 16384 | tf_op jit(solution)/shard_map/all_to_all | solution.py:178
  293.9 161.1 %all-to-all-start.3 = ((f32[2048,1,128]{2,1,0:T(1,128)}), f32[2048,1,128]{2,1,0:T(1,128)}, u32[]{:S(2)}, u32[]{:S(2)}) async-start(f32[2048,1,128]{2,1,0:T(1,128)} %broadcast_multiply_fusion.1), calls=%async_computation.3 | async-start | bytes 2097152 | tf_op jit(solution)/shard_map/all_to_all | solution.py:177
  346.7 1.9 copy-start.2
  349.5 6.5 %copy-start.3 = (f32[512,2048]{1,0:T(8,128)S(1)}, f32[512,2048]{1,0:T(8,128)}, u32[]{:S(2)}) copy-start(f32[512,2048]{1,0:T(8,128)} %copy-done.2) | copy-start | bytes 12582916 | tf_op jit(solution)/shard_map/while
  349.5 6.5 %copy-start.7 = (f32[2048,1,128]{2,1,0:T(1,128)S(1)}, f32[2048,1,128]{2,1,0:T(1,128)}, u32[]{:S(2)}) copy-start(f32[2048,1,128]{2,1,0:T(1,128)} %get-tuple-element.387) | copy-start | bytes 3145732 | tf_op jit(solution)/shard_map/while
  362.9 4.2 copy-start.5
  373.0 1.9 copy-start.2
  375.8 6.8 %copy-start.3 = (f32[512,2048]{1,0:T(8,128)S(1)}, f32[512,2048]{1,0:T(8,128)}, u32[]{:S(2)}) copy-start(f32[512,2048]{1,0:T(8,128)} %copy-done.2) | copy-start | bytes 12582916 | tf_op jit(solution)/shard_map/while
  375.8 6.8 %copy-start.7 = (f32[2048,1,128]{2,1,0:T(1,128)S(1)}, f32[2048,1,128]{2,1,0:T(1,128)}, u32[]{:S(2)}) copy-start(f32[2048,1,128]{2,1,0:T(1,128)} %get-tuple-element.387) | copy-start | bytes 3145732 | tf_op jit(solution)/shard_map/while
  389.6 4.2 copy-start.5
  399.7 1.9 copy-start.2
  402.4 6.8 %copy-start.3 = (f32[512,2048]{1,0:T(8,128)S(1)}, f32[512,2048]{1,0:T(8,128)}, u32[]{:S(2)}) copy-start(f32[512,2048]{1,0:T(8,128)} %copy-done.2) | copy-start | bytes 12582916 | tf_op jit(solution)/shard_map/while
  402.4 6.8 %copy-start.7 = (f32[2048,1,128]{2,1,0:T(1,128)S(1)}, f32[2048,1,128]{2,1,0:T(1,128)}, u32[]{:S(2)}) copy-start(f32[2048,1,128]{2,1,0:T(1,128)} %get-tuple-element.387) | copy-start | bytes 3145732 | tf_op jit(solution)/shard_map/while
  416.2 4.2 copy-start.5
  426.3 1.9 copy-start.2
  429.0 6.8 %copy-start.3 = (f32[512,2048]{1,0:T(8,128)S(1)}, f32[512,2048]{1,0:T(8,128)}, u32[]{:S(2)}) copy-start(f32[512,2048]{1,0:T(8,128)} %copy-done.2) | copy-start | bytes 12582916 | tf_op jit(solution)/shard_map/while
  429.1 6.8 %copy-start.7 = (f32[2048,1,128]{2,1,0:T(1,128)S(1)}, f32[2048,1,128]{2,1,0:T(1,128)}, u32[]{:S(2)}) copy-start(f32[2048,1,128]{2,1,0:T(1,128)} %get-tuple-element.387) | copy-start | bytes 3145732 | tf_op jit(solution)/shard_map/while
  442.8 4.2 copy-start.5
  455.1 104.8 %all-to-all-start.6 = ((f32[2048,3,1,128]{3,2,1,0:T(1,128)}), f32[2048,3,1,128]{3,2,1,0:T(1,128)}, u32[]{:S(2)}, u32[]{:S(2)}) async-start(f32[2048,3,1,128]{3,2,1,0:T(1,128)} %pad_maximum_fusion), calls=%async_computation.6 | async-start | bytes 6291456 | tf_op jit(solution)/shard_map/all_to_all | solution.py:190
  459.5 174.3 %all-reduce.3.cloned.1.call-start = ((), (), s32[]{:S(2)}) async-start(), calls=%async_computation.8 | async-start | bytes 4194304 | tf_op jit(solution)/shard_map/psum | solution.py:193
  559.8 77.2 %copy-start.1 = (f32[1,128,6144]{2,1,0:T(8,128)S(1)}, f32[1,128,6144]{2,1,0:T(8,128)}, u32[]{:S(2)}) copy-start(f32[1,128,6144]{2,1,0:T(8,128)} %param.12) | copy-start | bytes 9437188
Sparse Core Ops, SparseCore 0:
  465.8 168.0 all-reduce.2
where the time goes:
time: 654 us; the launch traced here: 644 us
  waiting for transfers between devices  210 us (32%)
  blocking collectives  118 us (18%)
  matrix products  107 us (16%)
  local copies, waits for them, and re-layouts  98.7 us (15%)
  starting transfers between devices  49.5 us (8%)
  other arithmetic  31.8 us (5%)
  between operations  15.3 us (2%)
  loops' own time  13.3 us (2%)
    psum x1, blocking collectives, body(): lax.psum((jnp.sum(onehot * excess[:, None], axis=0), jnp.sum(onehot, axis...  93.7 us
    all_to_all x1, waiting for transfers between devices, body(): lax.all_to_all(packed[0], 'seq', split_axis=0, concat_axis=0, tiled=True)  85.1 us
    psum x1, waiting for transfers between devices, body(): lax.psum(jnp.dot(embedding.T, gain_part[None, :], precision=highest), ('s...  64.3 us
    dot_general x8, matrix products, block_probs(): jnp.einsum('qhd,khd->hqk', query_rows, key_all, precision=highest)  35 us
    unnamed x20, local copies, waits for them, and re-layouts  32.4 us
    all_to_all x1, waiting for transfers between devices, body(): lax.all_to_all(seq_rows.reshape(local_rows, 3, HEADS, HEAD_DIM), 'seq', s...  32.4 us
    dot_general x4, matrix products, block_step(): jnp.einsum('hqk,qhd->khd', probability, upstream_rows, precision=highest)  26.7 us
    all_gather x1, blocking collectives, body(): all_weights = lax.all_gather(row_weight, 'seq', axis=0, tiled=True)  24.5 us
  transfers between devices with their start and end apart: 9, of which 7 were waited for; matrix products, arithmetic and copies ran while one was open for 25% of the time, Pallas kernels for 0%

commit v1 on v0

v1 whole, which is shorter than its diff:
```python
import functools
import math

import jax
import jax.numpy as jnp
import numpy as np
from jax import lax
from jax.experimental import pallas as pl
from jax.experimental.pallas import tpu as pltpu
from jax.sharding import PartitionSpec as P

HEADS = 16
DIM = 128
FREQ_DIM = 256
BUCKETS = 16
WIDTH = HEADS * DIM
RATE = 10.0
CHUNK = 64
LOG2E = 1.4426950408889634
SCALE = DIM ** (-0.5)
MESH = pl.DeviceIdType.MESH
HIGHEST = lax.Precision.HIGHEST
BF16 = jnp.bfloat16
F32 = jnp.float32

OFFSETS = (
    (0, 2), (2, 0), (2, 2), (1, 2), (-1, 2), (2, 1), (2, -1),
    (1, 1), (-1, -1), (1, -1), (-1, 1), (0, 1), (1, 0), (0, -1), (-1, 0),
)
POS, WEIGHT, BUCKET, REF, EMB, MIX = 0, 1, 2, 3, 4, 6
KEY, QUERY, VALUE, AIM = 0, 1, 2, 3
SLOT = {AIM: KEY, VALUE: QUERY, QUERY: VALUE, KEY: AIM}
PART_COLUMN = {KEY: WIDTH, QUERY: 0, VALUE: 2 * WIDTH, AIM: 0}


def split(x):
    hi = x.astype(BF16)
    return hi, (x - hi.astype(F32)).astype(BF16)


def dot(a, b):
    return lax.dot_general(a, b, (((1,), (0,)), ((), ())), preferred_element_type=F32)


def dot_nt(a, b):
    return lax.dot_general(a, b, (((1,), (1,)), ((), ())), preferred_element_type=F32)


def kernel(
    shards, copies, rows, aims, places, buckets, ref_row, steps, old, frequency, mod_w,
    att_out, grad_out, weight_out, mix_out,
    meta, meta_all, got, mod_buf, perm, cat, k3, kt, q3, v3, vt, u3, e_hi, e_lo, head_out, inv_sum, delta,
    gain_sum, score_a, score_b, loss_rows, stage1, tile1, stage2, tile2, stage3, tile3,
    send_sem, recv_sem, back_send, back_recv, small_send, small_recv, mod_sem,
):
    length = shards * DIM
    me = lax.axis_index("seq")
    sample = lax.axis_index("dp")
    my_z, my_y = me // 4, lax.rem(me, 4)

    def peer(step):
        return lax.rem(my_z + step[0] + 4, 4) * 4 + lax.rem(my_y + step[1] + 4, 4)

    barrier = pltpu.get_barrier_semaphore()
    for step in OFFSETS:
        pl.semaphore_signal(barrier, inc=1, device_id={"seq": peer(step)}, device_id_type=MESH)
    for turn in range(1, copies):
        other = lax.rem(sample + turn, copies)
        pl.semaphore_signal(barrier, inc=1, device_id={"dp": other}, device_id_type=MESH)

    meta[POS : POS + 1, :] = places[...].astype(F32)
    bucket_row = buckets[...]
    lane = lax.broadcasted_iota(jnp.int32, (1, DIM), 1)
    weight_row = jnp.zeros((1, DIM), F32)
    old_row = jnp.zeros((1, DIM), F32)
    for bucket in range(BUCKETS):
        weight_row = weight_row + jnp.where(bucket_row == bucket, old[bucket], 0.0)
        old_row = old_row + jnp.where(lane == bucket, old[bucket], 0.0)
    meta[WEIGHT : WEIGHT + 1, :] = weight_row
    meta[BUCKET : BUCKET + 1, :] = bucket_row.astype(F32)
    meta[REF : REF + 1, :] = ref_row[...]
    angles = steps[0].astype(F32) * frequency[...]
    for row, wave in ((EMB, jnp.cos(angles)), (EMB + 1, jnp.sin(angles))):
        meta[row : row + 1, :] = wave / (1.0 + jnp.exp(-wave))
    meta[MIX : MIX + 1, :] = old_row
    meta[MIX + 1 : MIX + 2, :] = jnp.zeros((1, DIM), F32)
    pl.semaphore_wait(barrier, shards - 1 + copies - 1)

    meta_all[me] = meta[...]
    for step in OFFSETS:
        pltpu.make_async_remote_copy(
            meta, meta_all.at[me], small_send.at[0], small_recv.at[0],
            device_id={"seq": peer(step)}, device_id_type=MESH,
        ).start()
    mod_copy = pltpu.make_async_copy(
        mod_w.at[:, pl.ds(pl.multiple_of(me * DIM, DIM), DIM)], mod_buf, mod_sem
    )
    mod_copy.start()

    def source(part, head):
        base = aims if part == AIM else rows
        return base.at[:, pl.ds(pl.multiple_of(PART_COLUMN[part] + head * DIM, DIM), DIM)]

    def landing(part):
        return got.at[part, pl.ds(pl.multiple_of(me * DIM, DIM), DIM), :]

    for part in (KEY, QUERY, VALUE, AIM):
        pltpu.make_async_copy(source(part, me), landing(part), recv_sem.at[part]).start()
        for step in OFFSETS:
            head = peer(step)
            pltpu.make_async_remote_copy(
                source(part, head), landing(part), send_sem.at[part], recv_sem.at[part],
                device_id={"seq": head}, device_id_type=MESH,
            ).start()

    def wait_small(stage, buffer, count):
        pltpu.make_async_copy(buffer.at[pl.ds(0, count)], buffer.at[pl.ds(0, count)], small_recv.at[stage]).wait()

    def wait_small_send(stage, buffer, count):
        pltpu.make_async_copy(buffer.at[pl.ds(0, count)], buffer.at[pl.ds(0, count)], small_send.at[stage]).wait()

    mod_copy.wait()
    embedding = jnp.concatenate([meta[EMB : EMB + 1, :], meta[EMB + 1 : EMB + 2, :]], axis=1)
    embedding = jnp.broadcast_to(embedding, (8, FREQ_DIM))
    gain_row = 1.0 + lax.dot_general(
        embedding, mod_buf[...], (((1,), (0,)), ((), ())), precision=HIGHEST, preferred_element_type=F32
    )
    gain = jnp.broadcast_to(gain_row[0:1, :], (DIM, DIM)).T

    wait_small(0, meta_all, shards - 1)

    def perm_block(block, carry):
        at = pl.multiple_of(block * 256, 256)
        place = (lax.broadcasted_iota(jnp.int32, (256, DIM), 0) + at).astype(F32)
        for shard in range(shards):
            hit = place == meta_all[shard, POS : POS + 1, :]
            perm[pl.ds(at, 256), shard * DIM : (shard + 1) * DIM] = jnp.where(hit, 1.0, 0.0).astype(BF16)
        return carry

    lax.fori_loop(0, length // 256, perm_block, 0)

    def pipeline(count, make, use, finish=None):
        def both(at, last):
            make(at + 1, score_b)
            use(at, score_a)
            if not last:
                make(at + 2, score_a)
            use(at + 1, score_b)
            if finish is not None:
                finish(at)
                finish(at + 1)

        def one(pair, carry):
            both(2 * pair, False)
            return carry

        make(0, score_a)
        lax.fori_loop(0, count // 2 - 1, one, 0)
        both(count - 2, True)

    def arrive(part, factor):
        pltpu.make_async_copy(got.at[part], got.at[part], recv_sem.at[part]).wait()

        def one(block, carry):
            at = pl.multiple_of(block * 256, 256)
            hi, lo = split(got[part, pl.ds(at, 256), :] * factor)
            cat[pl.ds(at, 256), 0:DIM] = hi
            cat[pl.ds(at, 256), DIM : 2 * DIM] = lo
            return carry

        lax.fori_loop(0, length // 256, one, 0)

    def reorder(part, factor, into, transposed):
        arrive(part, factor)

        def make(block, buffer):
            at = pl.multiple_of(block * 512, 512)
            buffer[0:512, :] = dot(perm[pl.ds(at, 512), :], cat[...])

        def use(block, buffer):
            at = pl.multiple_of(block * 512, 512)
            placed = buffer[0:512, :]
            hi, lo = placed[:, :DIM].astype(BF16), placed[:, DIM:].astype(BF16)
            into[pl.ds(at, 512), 0:DIM] = hi
            into[pl.ds(at, 512), DIM : 2 * DIM] = hi if part == QUERY else lo
            into[pl.ds(at, 512), 2 * DIM : 3 * DIM] = lo if part == QUERY else hi
            if transposed is not None:
                hi, lo = split((placed[:, :DIM] + placed[:, DIM:]).T)
                transposed[0:DIM, pl.ds(at, 512)] = hi
                transposed[DIM : 2 * DIM, pl.ds(at, 512)] = lo

        pipeline(length // 512, make, use)

    def by_columns(left, high, low):
        full = dot(left[...], high)
        return full[:DIM] + full[DIM:] + dot(left[0:DIM, :], low)

    def by_rows(at, right):
        full = dot(e_hi[pl.ds(at, 512), :], right[...])
        return full[:, :DIM] + full[:, DIM:] + dot(e_lo[pl.ds(at, 512), :], right[:, 0:DIM])

    reorder(KEY, 1.0, k3, kt)
    reorder(QUERY, SCALE * LOG2E, q3, None)

    def score_block(block, buffer):
        at = pl.multiple_of(block * 256, 256)
        buffer[...] = dot_nt(k3[...], q3[pl.ds(at, 256), :])

    def softmax_block(block, buffer):
        at = pl.multiple_of(block * 256, 256)
        top = jnp.full((8, 256), -jnp.inf, F32)
        for row in range(0, length, CHUNK):
            top = jnp.maximum(top, jnp.max(buffer[row : row + CHUNK, :].reshape(CHUNK // 8, 8, 256), axis=0))
        top = jnp.max(top, axis=0, keepdims=True)
        sums = jnp.zeros((8, 256), F32)
        for row in range(0, length, CHUNK):
            weights = jnp.exp2(buffer[row : row + CHUNK, :] - top)
            sums = sums + jnp.sum(weights.reshape(CHUNK // 8, 8, 256), axis=0)
            hi, lo = split(weights)
            e_hi[row : row + CHUNK, pl.ds(at, 256)] = hi
            e_lo[row : row + CHUNK, pl.ds(at, 256)] = lo
        inv_sum[:, pl.ds(at, 256)] = jnp.broadcast_to(1.0 / jnp.sum(sums, axis=0, keepdims=True), (8, 256))

    pipeline(length // 256, score_block, softmax_block)

    def target(part):
        base = att_out if part == AIM else grad_out
        return base.at[:, pl.ds(pl.multiple_of(PART_COLUMN[part] + me * DIM, DIM), DIM)]

    def give(part, shard):
        block = got.at[SLOT[part], pl.ds(pl.multiple_of(shard * DIM, DIM), DIM), :]

        @pl.when(shard != me)
        def _():
            pltpu.make_async_remote_copy(
                block, target(part), back_send.at[part], back_recv.at[part],
                device_id={"seq": shard}, device_id_type=MESH,
            ).start()

        @pl.when(shard == me)
        def _():
            pltpu.make_async_copy(block, target(part), back_recv.at[part]).start()

    def pair_of(turn):
        return lax.rem(my_z + 2 + turn // 2, 4) * 2 + lax.rem(my_y // 2 + 1 + lax.rem(turn, 2), 2)

    def row_of(turn):
        return lax.rem(my_z + 2 + turn, 4)

    reorder(VALUE, 1.0, v3, vt)

    def output_block(turn, buffer):
        at = pl.multiple_of(pair_of(turn) * 256, 256)
        buffer[0:DIM, :] = by_columns(vt, e_hi[:, pl.ds(at, 256)], e_lo[:, pl.ds(at, 256)])

    def attended_block(turn, buffer):
        at = pl.multiple_of(pair_of(turn) * 256, 256)
        out = buffer[0:DIM, :] * inv_sum[0:1, pl.ds(at, 256)]
        head_out[:, pl.ds(at, 256)] = out
        for half in range(2):
            begin = pl.multiple_of(at + half * DIM, DIM)
            got[SLOT[AIM], pl.ds(begin, DIM), :] = (gain * out[:, half * DIM : (half + 1) * DIM]).T

    def give_pair(part):
        def finish(turn):
            for half in range(2):
                give(part, pair_of(turn) * 2 + half)

        return finish

    pipeline(shards // 2, output_block, attended_block, give_pair(AIM))

    arrive(AIM, 1.0)

    def aim_block(block, buffer):
        at = pl.multiple_of(block * 512, 512)
        buffer[0:512, :] = dot(perm[pl.ds(at, 512), :], cat[...])

    gain_sum[...] = jnp.zeros((DIM, DIM), F32)

    def upstream_block(block, buffer):
        at = pl.multiple_of(block * 512, 512)
        placed = buffer[0:512, :]
        aim = placed[:, :DIM] + placed[:, DIM:]
        total = jnp.zeros((DIM, DIM), F32)
        for quarter in range(4):
            shard = block * 4 + quarter
            begin = pl.multiple_of(at + quarter * DIM, DIM)
            out = head_out[:, pl.ds(begin, DIM)]
            gap = gain * out - aim[quarter * DIM : (quarter + 1) * DIM, :].T
            loss_rows[shard] = jnp.broadcast_to(jnp.sum(gap * gap, axis=0, keepdims=True), (8, DIM))
            up_a = gap * meta_all[shard, WEIGHT : WEIGHT + 1, :]
            total = total + up_a * out
            up = gain * up_a * inv_sum[0:1, pl.ds(begin, DIM)]
            delta[:, pl.ds(begin, DIM)] = jnp.broadcast_to(jnp.sum(up * out, axis=0, keepdims=True), (8, DIM))
            hi, lo = split(up.T)
            u3[pl.ds(begin, DIM), 0:DIM] = hi
            u3[pl.ds(begin, DIM), DIM : 2 * DIM] = hi
            u3[pl.ds(begin, DIM), 2 * DIM : 3 * DIM] = lo
        gain_sum[...] += total

    pipeline(length // 512, aim_block, upstream_block)

    gain_grad = jnp.sum(gain_sum[...].T, axis=0, keepdims=True)
    row_index = lax.broadcasted_iota(jnp.int32, (8, DIM), 0)
    for shard in range(shards):
        tile1[shard] = jnp.where(row_index == 0, loss_rows[shard], jnp.broadcast_to(gain_grad, (8, DIM)))
    stage1[me] = tile1[me]
    for step in OFFSETS:
        shard = peer(step)
        pltpu.make_async_remote_copy(
            tile1.at[shard], stage1.at[me], small_send.at[1], small_recv.at[1],
            device_id={"seq": shard}, device_id_type=MESH,
        ).start()

    def value_grad_block(turn, carry):
        block = row_of(turn)
        at = pl.multiple_of(block * 512, 512)
        got[SLOT[VALUE], pl.ds(at, 512), :] = by_rows(at, u3.at[:, DIM : 3 * DIM])
        for quarter in range(4):
            give(VALUE, block * 4 + quarter)
        return carry

    lax.fori_loop(0, shards // 4, value_grad_block, 0)

    hi_a, lo_a, hi_b, lo_b = (perm.at[:, at : at + 256] for at in range(0, 1024, 256))

    def prob_grad_block(turn, buffer):
        at = pl.multiple_of(pair_of(turn) * 256, 256)
        buffer[...] = dot_nt(v3[...], u3[pl.ds(at, 256), :])

    def score_grad_block(turn, buffer, high, low):
        at = pl.multiple_of(pair_of(turn) * 256, 256)
        shift = delta[0:1, pl.ds(at, 256)]
        for row in range(0, length, CHUNK):
            here = (slice(row, row + CHUNK), pl.ds(at, 256))
            weights = e_hi[here].astype(F32) + e_lo[here].astype(F32)
            hi, lo = split((buffer[row : row + CHUNK, :] - shift) * weights)
            high[row : row + CHUNK, :] = hi
            low[row : row + CHUNK, :] = lo
            e_hi[here] = hi
            e_lo[here] = lo

    def query_grad_block(turn, high, low):
        at = pl.multiple_of(pair_of(turn) * 256, 256)
        grad = by_columns(kt, high[...], low[...]) * SCALE
        for half in range(2):
            begin = pl.multiple_of(at + half * DIM, DIM)
            got[SLOT[QUERY], pl.ds(begin, DIM), :] = grad[:, half * DIM : (half + 1) * DIM].T

    give_queries = give_pair(QUERY)
    prob_grad_block(0, score_a)
    prob_grad_block(1, score_b)
    score_grad_block(0, score_a, hi_a, lo_a)

    def gradient_pair(pair, carry):
        turn = 2 * pair + 1
        prob_grad_block(turn + 1, score_a)
        score_grad_block(turn, score_b, hi_b, lo_b)
        query_grad_block(turn - 1, hi_a, lo_a)
        prob_grad_block(turn + 2, score_b)
        score_grad_block(turn + 1, score_a, hi_a, lo_a)
        query_grad_block(turn, hi_b, lo_b)
        give_queries(turn - 1)
        give_queries(turn)
        return carry

    last = shards // 2 - 1
    lax.fori_loop(0, last // 2, gradient_pair, 0)
    score_grad_block(last, score_b, hi_b, lo_b)
    query_grad_block(last - 1, hi_a, lo_a)
    query_grad_block(last, hi_b, lo_b)
    give_queries(last - 1)
    give_queries(last)

    wait_small(1, stage1, shards - 1)
    loss = jnp.zeros((1, DIM), F32)
    for shard in range(shards):
        loss = loss + stage1[shard, 0:1, :]
    excess = jnp.maximum(0.5 * loss / WIDTH - meta[REF : REF + 1, :], 0.0)
    hit = lax.broadcasted_iota(jnp.int32, (DIM, DIM), 0).astype(F32) == meta[BUCKET : BUCKET + 1, :]
    sums = lax.dot_general(
        jnp.where(row_index == 0, jnp.broadcast_to(excess, (8, DIM)), 1.0), jnp.where(hit, 1.0, 0.0),
        (((1,), (1,)), ((), ())), precision=HIGHEST, preferred_element_type=F32,
    )
    for shard in range(shards):
        tile2[shard : shard + 1, :] = stage1[shard, 1:2, :]
    tile2[shards : shards + 8, :] = sums
    tile2[shards + 2 : shards + 4, :] = meta[EMB : EMB + 2, :]
    stage2[sample] = tile2[...]
    for turn in range(1, copies):
        other = lax.rem(sample + turn, copies)
        pltpu.make_async_remote_copy(
            tile2, stage2.at[sample], small_send.at[2], small_recv.at[2],
            device_id={"dp": other}, device_id_type=MESH,
        ).start()

    def key_grad_block(turn, carry):
        block = row_of(turn)
        at = pl.multiple_of(block * 512, 512)
        got[SLOT[KEY], pl.ds(at, 512), :] = by_rows(at, q3.at[:, DIM : 3 * DIM]) * (1.0 / LOG2E)
        for quarter in range(4):
            give(KEY, block * 4 + quarter)
        return carry

    lax.fori_loop(0, shards // 4, key_grad_block, 0)

    if copies > 1:
        wait_small(2, stage2, copies - 1)
    sums = jnp.zeros((8, DIM), F32)
    for other in range(copies):
        sums = sums + stage2[other, shards : shards + 8, :]
    tile3[...] = sums
    stage3[me] = sums
    for step in OFFSETS:
        pltpu.make_async_remote_copy(
            tile3, stage3.at[me], small_send.at[3], small_recv.at[3],
            device_id={"seq": peer(step)}, device_id_type=MESH,
        ).start()

    by_sample = jnp.concatenate(
        [
            jnp.concatenate([stage2[other, row : row + 1, :] for row in (shards + 2, shards + 3)], axis=1)
            for other in range(copies)
        ],
        axis=0,
    )
    by_frequency = by_sample.T
    for head in range(shards):
        gains = jnp.concatenate([stage2[other, head : head + 1, :] for other in range(copies)], axis=0)
        weight_out[:, head * DIM : (head + 1) * DIM] = lax.dot_general(
            by_frequency, gains, (((1,), (0,)), ((), ())), precision=HIGHEST, preferred_element_type=F32
        )
    wait_small(3, stage3, shards - 1)
    sums = jnp.zeros((8, DIM), F32)
    for shard in range(shards):
        sums = sums + stage3[shard]
    mean = sums[0:1, :] / jnp.maximum(sums[1:2, :], 1.0)
    updated = meta[MIX : MIX + 1, :] * (1.0 + RATE * mean)
    updated = jnp.where(lane < BUCKETS, updated, 0.0)
    mixture = BUCKETS * updated / jnp.sum(updated, axis=1, keepdims=True)
    mix_out[...] = mixture[:, :BUCKETS]

    others = (shards - 1) * DIM
    for part in (KEY, QUERY, VALUE, AIM):
        sent = got.at[part, pl.ds(0, others), :]
        pltpu.make_async_copy(sent, sent, send_sem.at[part]).wait()
        sent = got.at[SLOT[part], pl.ds(0, others), :]
        pltpu.make_async_copy(sent, sent, back_send.at[part]).wait()
        base = att_out if part == AIM else grad_out
        landed = base.at[:, PART_COLUMN[part] : PART_COLUMN[part] + WIDTH]
        pltpu.make_async_copy(landed, landed, back_recv.at[part]).wait()
    wait_small_send(0, meta_all, shards - 1)
    wait_small_send(1, stage1, shards - 1)
    if copies > 1:
        wait_small_send(2, stage2, copies - 1)
    wait_small_send(3, stage3, shards - 1)


def body(reader_rows, reader_targets, dest_pos, bucket_ids, ref_loss, timesteps, mod_weight, mixture_old):
    shards, copies = lax.axis_size("seq"), lax.axis_size("dp")
    length = shards * DIM
    half = FREQ_DIM // 2
    frequency = np.exp(-math.log(10000.0) * np.arange(half) / half).astype(np.float32)[None, :]
    any_spec = pl.BlockSpec(memory_space=pl.ANY)
    vmem_spec = pl.BlockSpec(memory_space=pltpu.VMEM)
    dma = pltpu.SemaphoreType.DMA
    smem_spec = pl.BlockSpec(memory_space=pltpu.SMEM)
    attended, grads, weight_grad, mixture = pl.pallas_call(
        functools.partial(kernel, shards, copies),
        out_shape=(
            pltpu.VMEM((DIM, WIDTH), F32),
            pltpu.VMEM((DIM, 3 * WIDTH), F32),
            pltpu.VMEM((FREQ_DIM, WIDTH), F32),
            jax.ShapeDtypeStruct((1, BUCKETS), F32),
        ),
        in_specs=[any_spec, any_spec, vmem_spec, vmem_spec, vmem_spec, smem_spec, smem_spec, vmem_spec, any_spec],
        out_specs=(vmem_spec, vmem_spec, vmem_spec, vmem_spec),
        scratch_shapes=[
            pltpu.VMEM((8, DIM), F32),
            pltpu.VMEM((shards, 8, DIM), F32),
            pltpu.VMEM((4, length, DIM), F32),
            pltpu.VMEM((FREQ_DIM, DIM), F32),
            pltpu.VMEM((length, length), BF16),
            pltpu.VMEM((length, 2 * DIM), BF16),
            pltpu.VMEM((length, 3 * DIM), BF16),
            pltpu.VMEM((2 * DIM, length), BF16),
            pltpu.VMEM((length, 3 * DIM), BF16),
            pltpu.VMEM((length, 3 * DIM), BF16),
            pltpu.VMEM((2 * DIM, length), BF16),
            pltpu.VMEM((length, 3 * DIM), BF16),
            pltpu.VMEM((length, length), BF16),
            pltpu.VMEM((length, length), BF16),
            pltpu.VMEM((DIM, length), F32),
            pltpu.VMEM((8, length), F32),
            pltpu.VMEM((8, length), F32),
            pltpu.VMEM((DIM, DIM), F32),
            pltpu.VMEM((length, 256), F32),
            pltpu.VMEM((length, 256), F32),
            pltpu.VMEM((shards, 8, DIM), F32),
            pltpu.VMEM((shards, 8, DIM), F32),
            pltpu.VMEM((shards, 8, DIM), F32),
            pltpu.VMEM((copies, shards + 8, DIM), F32),
            pltpu.VMEM((shards + 8, DIM), F32),
            pltpu.VMEM((shards, 8, DIM), F32),
            pltpu.VMEM((8, DIM), F32),
            dma((4,)), dma((4,)), dma((4,)), dma((4,)), dma((4,)), dma((4,)), dma,
        ],
        compiler_params=pltpu.CompilerParams(
            collective_id=0, has_side_effects=True, vmem_limit_bytes=56 * 1024 * 1024
        ),
        name="attend",
    )(reader_rows[0], reader_targets[0], dest_pos, bucket_ids, ref_loss, timesteps, mixture_old, frequency, mod_weight)
    return attended[None], grads[None], weight_grad, mixture[0]


def solution(mesh):
    return jax.shard_map(
        body,
        mesh=mesh,
        in_specs=(
            P("dp", "seq", None), P("dp", "seq", None), P("dp", "seq"), P("dp", "seq"),
            P("dp", "seq"), P("dp"), P(), P(),
        ),
        out_specs=(P("dp", "seq", None), P("dp", "seq", None), P(), P()),
        check_vma=False,
    )
```

time: 654 us -> 115 us (0.18); the launches traced: 644 us -> 114 us
  waiting for transfers between devices: 210 us -> 0 us
  blocking collectives: 118 us -> 0 us
  Pallas kernels: 0 us -> 108 us
  matrix products: 107 us -> 0 us
  local copies, waits for them, and re-layouts: 98.7 us -> 4.47 us
  starting transfers between devices: 49.5 us -> 0 us
  other arithmetic: 31.8 us -> 0 us
  between operations: 15.3 us -> 1.29 us
  loops' own time: 13.3 us -> 0 us
    all_to_all x8 -> x0, waiting for transfers between devices: 146 us -> none  [the longest x1 85.1 us: body(): lax.all_to_all(packed[0], 'seq', split_axis=0, concat_axis=0, tiled=True)]
    pallas_call x0 -> x1, Pallas kernels: none -> 108 us  [body(): pl.pallas_call(functools.partial(kernel, shards, copies), out_shape=(pltp...]
    dot_general x25 -> x0, matrix products: 107 us -> none  [the longest x8 35 us: block_probs(): jnp.einsum('qhd,khd->hqk', query_rows, key_all, precision=highest)]
    psum x1 -> x0, blocking collectives: 93.7 us -> none  [body(): lax.psum((jnp.sum(onehot * excess[:, None], axis=0), jnp.sum(onehot, axis...]
    psum x1 -> x0, waiting for transfers between devices: 64.3 us -> none  [body(): lax.psum(jnp.dot(embedding.T, gain_part[None, :], precision=highest), ('s...]
    all_to_all x8 -> x0, starting transfers between devices: 49.5 us -> none  [the longest x1 9.31 us: body(): lax.all_to_all(partial_loss[:, None], 'seq', split_axis=0, concat_axis=1,...]
    unnamed x20 -> x6, local copies, waits for them, and re-layouts: 32.4 us -> 4.47 us
    all_gather x1 -> x0, blocking collectives: 24.5 us -> none  [body(): all_weights = lax.all_gather(row_weight, 'seq', axis=0, tiled=True)]
  transfers between devices with their start and end apart: 9 -> 0, of which waited for: 7 -> 0; matrix products, arithmetic and copies ran while one was open for 25% -> 0% of each run, Pallas kernels for 0% -> 0%
where the time goes in v1:
time: 115 us; the launch traced here: 114 us
  Pallas kernels  108 us (94%)
  local copies, waits for them, and re-layouts  4.47 us (4%)
  between operations  1.29 us (1%)
    pallas_call x1, Pallas kernels, body(): pl.pallas_call(functools.partial(kernel, shards, copies), out_shape=(pltp...  108 us
    unnamed x6, local copies, waits for them, and re-layouts  4.47 us

profile of v1, /device:TPU:1, one launch (start us, length us, event | category | flops | bytes accessed | tf_op | source)
XLA Modules:
  0.0 114.1 jit_solution(16986665118321222069)
XLA Ops:
  1.3 108.3 %attend.1 = (f32[128,2048]{1,0:T(8,128)S(1)}, f32[128,6144]{1,0:T(8,128)S(1)}, f32[256,2048]{1,0:T(8,128)S(1)}, f32[1,16]{1,0:T(1,128)}) custom-call(f32[128,6144]{1,0:T(8,128)} %bitcast.7, f32[128,2048]{1,0:T(8,128)} %bitcast.8, s32[1,128]{1,0:T(1,128)} %places.1, s32[1,128]{1,0:T(1,128)} %buckets.1, f32[1,128]{1,0:T(1,128)} %ref_row.1, s32[1]{0:T(128)S(6)} %copy.20.steps, ...), custom_call_target="tpu_custom_call" | custom-call | tf_op jit(solution)/shard_map/attend/pallas_call | solution.py:469
  109.6 1.0 copy.17
  110.6 1.7 %copy.18 = f32[1,128,6144]{2,1,0:T(8,128)} copy(f32[1,128,6144]{2,1,0:T(8,128)S(1)} %bitcast.5) | data formatting | bytes 6291456
  112.3 0.0 copy-start
  112.3 1.3 %copy.19 = f32[256,2048]{1,0:T(8,128)} copy(f32[256,2048]{1,0:T(8,128)S(1)} %get-tuple-element.14) | data formatting | bytes 4194304
  113.6 0.0 copy-done
  113.6 0.5 copy.21
Async XLA Ops:
  112.3 1.3 %copy-start = (f32[1,16]{1,0:T(1,128)S(1)}, f32[1,16]{1,0:T(1,128)}, u32[]{:S(2)}) copy-start(f32[1,16]{1,0:T(1,128)} %get-tuple-element.11) | copy-start | bytes 196

commit v2 on v1

--- a/solution.py
+++ b/solution.py
@@ -24,8 +24,8 @@
 F32 = jnp.float32
 
 OFFSETS = (
-    (0, 2), (2, 0), (2, 2), (1, 2), (-1, 2), (2, 1), (2, -1),
-    (1, 1), (-1, -1), (1, -1), (-1, 1), (0, 1), (1, 0), (0, -1), (-1, 0),
+    (0, 1), (1, 0), (0, -1), (-1, 0), (1, 1), (-1, -1), (1, -1), (-1, 1),
+    (0, 2), (2, 0), (1, 2), (2, 1), (-1, 2), (2, -1), (2, 2),
 )
 POS, WEIGHT, BUCKET, REF, EMB, MIX = 0, 1, 2, 3, 4, 6
 KEY, QUERY, VALUE, AIM = 0, 1, 2, 3
@@ -58,8 +58,10 @@
     sample = lax.axis_index("dp")
     my_z, my_y = me // 4, lax.rem(me, 4)
 
+    side = 1 - 2 * lax.rem(sample, 2)
+
     def peer(step):
-        return lax.rem(my_z + step[0] + 4, 4) * 4 + lax.rem(my_y + step[1] + 4, 4)
+        return lax.rem(my_z + side * step[0] + 4, 4) * 4 + lax.rem(my_y + side * step[1] + 4, 4)
 
     barrier = pltpu.get_barrier_semaphore()
     for step in OFFSETS:
@@ -104,7 +106,7 @@
     def landing(part):
         return got.at[part, pl.ds(pl.multiple_of(me * DIM, DIM), DIM), :]
 
-    for part in (KEY, QUERY, VALUE, AIM):
+    def send(part):
         pltpu.make_async_copy(source(part, me), landing(part), recv_sem.at[part]).start()
         for step in OFFSETS:
             head = peer(step)
@@ -112,6 +114,13 @@
                 source(part, head), landing(part), send_sem.at[part], recv_sem.at[part],
                 device_id={"seq": head}, device_id_type=MESH,
             ).start()
+
+    def wait_sent(part):
+        sent = got.at[part, pl.ds(0, (shards - 1) * DIM), :]
+        pltpu.make_async_copy(sent, sent, send_sem.at[part]).wait()
+
+    send(KEY)
+    send(QUERY)
 
     def wait_small(stage, buffer, count):
         pltpu.make_async_copy(buffer.at[pl.ds(0, count)], buffer.at[pl.ds(0, count)], small_recv.at[stage]).wait()
@@ -199,7 +208,11 @@
         full = dot(e_hi[pl.ds(at, 512), :], right[...])
         return full[:, :DIM] + full[:, DIM:] + dot(e_lo[pl.ds(at, 512), :], right[:, 0:DIM])
 
+    wait_sent(KEY)
+    send(VALUE)
     reorder(KEY, 1.0, k3, kt)
+    wait_sent(QUERY)
+    send(AIM)
     reorder(QUERY, SCALE * LOG2E, q3, None)
 
     def score_block(block, buffer):
@@ -242,10 +255,10 @@
             pltpu.make_async_copy(block, target(part), back_recv.at[part]).start()
 
     def pair_of(turn):
-        return lax.rem(my_z + 2 + turn // 2, 4) * 2 + lax.rem(my_y // 2 + 1 + lax.rem(turn, 2), 2)
+        return lax.rem(my_z + 6 + side * (turn // 2), 4) * 2 + lax.rem(my_y // 2 + 1 + lax.rem(turn, 2), 2)
 
     def row_of(turn):
-        return lax.rem(my_z + 2 + turn, 4)
+        return lax.rem(my_z + 6 + side * turn, 4)
 
     reorder(VALUE, 1.0, v3, vt)
 
@@ -443,8 +456,8 @@
 
     others = (shards - 1) * DIM
     for part in (KEY, QUERY, VALUE, AIM):
-        sent = got.at[part, pl.ds(0, others), :]
-        pltpu.make_async_copy(sent, sent, send_sem.at[part]).wait()
+        if part in (VALUE, AIM):
+            wait_sent(part)
         sent = got.at[SLOT[part], pl.ds(0, others), :]
         pltpu.make_async_copy(sent, sent, back_send.at[part]).wait()
         base = att_out if part == AIM else grad_out
@@ -455,6 +468,22 @@
     if copies > 1:
         wait_small_send(2, stage2, copies - 1)
     wait_small_send(3, stage3, shards - 1)
+
+
+def move_out(*refs):
+    count = len(refs) // 2
+    sources, outputs, sems = refs[:count], refs[count : 2 * count], refs[-1]
+    moves = []
+    for source, output in zip(sources, outputs):
+        pieces = 4 if source.shape[0] >= DIM else 1
+        rows = source.shape[0] // pieces
+        for piece in range(pieces):
+            part = pl.ds(piece * rows, rows)
+            moves.append(pltpu.make_async_copy(source.at[part], output.at[part], sems.at[len(moves)]))
+    for move in moves:
+        move.start()
+    for move in moves:
+        move.wait()
 
 
 def body(reader_rows, reader_targets, dest_pos, bucket_ids, ref_loss, timesteps, mod_weight, mixture_old):
@@ -472,7 +501,7 @@
             pltpu.VMEM((DIM, WIDTH), F32),
             pltpu.VMEM((DIM, 3 * WIDTH), F32),
             pltpu.VMEM((FREQ_DIM, WIDTH), F32),
-            jax.ShapeDtypeStruct((1, BUCKETS), F32),
+            pltpu.VMEM((1, BUCKETS), F32),
         ),
         in_specs=[any_spec, any_spec, vmem_spec, vmem_spec, vmem_spec, smem_spec, smem_spec, vmem_spec, any_spec],
         out_specs=(vmem_spec, vmem_spec, vmem_spec, vmem_spec),
@@ -511,6 +540,15 @@
         ),
         name="attend",
     )(reader_rows[0], reader_targets[0], dest_pos, bucket_ids, ref_loss, timesteps, mixture_old, frequency, mod_weight)
+    results = (attended, grads, weight_grad, mixture)
+    attended, grads, weight_grad, mixture = pl.pallas_call(
+        move_out,
+        out_shape=tuple(jax.ShapeDtypeStruct(item.shape, F32) for item in results),
+        in_specs=[vmem_spec] * 4,
+        out_specs=(any_spec,) * 4,
+        scratch_shapes=[dma((13,))],
+        name="move_out",
+    )(*results)
     return attended[None], grads[None], weight_grad, mixture[0]
 
 

time: 115 us -> 123 us (1.070)
  Pallas kernels: 108 us -> 116 us
    pallas_call x0 -> x1, Pallas kernels: none -> 5.62 us  [body(): pl.pallas_call(move_out, out_shape=tuple((jax.ShapeDtypeStruct(item.shape...]
    pallas_call x1, Pallas kernels: 108 us -> 111 us  [body(): pl.pallas_call(functools.partial(kernel, shards, copies), out_shape=(pltp...]
    unnamed x6 -> x8, local copies, waits for them, and re-layouts: 4.47 us -> 4.56 us
where the time goes in v2:
time: 123 us
  Pallas kernels  116 us (94%)
  local copies, waits for them, and re-layouts  4.56 us (4%)
  between operations  1.48 us (1%)
    pallas_call x1, Pallas kernels, body(): pl.pallas_call(functools.partial(kernel, shards, copies), out_shape=(pltp...  111 us
    pallas_call x1, Pallas kernels, body(): pl.pallas_call(move_out, out_shape=tuple((jax.ShapeDtypeStruct(item.shape...  5.62 us
    unnamed x8, local copies, waits for them, and re-layouts  4.56 us

profile of v2, /device:TPU:1, one launch (start us, length us, event | category | flops | bytes accessed | tf_op | source)
XLA Modules:
  0.0 122.5 jit_solution(2154573957033038964)
XLA Ops:
  1.3 110.8 %attend.1 = (f32[128,2048]{1,0:T(8,128)S(1)}, f32[128,6144]{1,0:T(8,128)S(1)}, f32[256,2048]{1,0:T(8,128)S(1)}, f32[1,16]{1,0:T(1,128)S(1)}) custom-call(f32[128,6144]{1,0:T(8,128)} %bitcast.5, f32[128,2048]{1,0:T(8,128)} %bitcast.6, s32[1,128]{1,0:T(1,128)} %places.1, s32[1,128]{1,0:T(1,128)} %buckets.1, f32[1,128]{1,0:T(1,128)} %ref_row.1, ...), custom_call_target="tpu_custom_call" | custom-call | tf_op jit(solution)/shard_map/attend/pallas_call | solution.py:498
  112.1 0.0 copy-start
  112.1 1.6 %copy-done = f32[128,6144]{1,0:T(8,128)} copy-done((f32[128,6144]{1,0:T(8,128)}, f32[128,6144]{1,0:T(8,128)S(1)}, u32[]{:S(2)}) %copy-start) | copy-done | bytes 3145752
  113.8 0.0 copy-start.1
  113.8 1.3 %copy-done.1 = f32[256,2048]{1,0:T(8,128)} copy-done((f32[256,2048]{1,0:T(8,128)}, f32[256,2048]{1,0:T(8,128)S(1)}, u32[]{:S(2)}) %copy-start.1) | copy-done | bytes 2097176
  115.1 0.0 copy-start.2
  115.1 1.0 copy-done.2
  116.1 0.0 copy-start.3
  116.1 0.6 copy-done.3
  116.7 5.6 %move_out.1 = (f32[128,2048]{1,0:T(8,128)}, f32[128,6144]{1,0:T(8,128)}, f32[256,2048]{1,0:T(8,128)}, f32[1,16]{1,0:T(1,128)}) custom-call(f32[128,2048]{1,0:T(8,128)} %copy-done.2, f32[128,6144]{1,0:T(8,128)} %copy-done, f32[256,2048]{1,0:T(8,128)} %copy-done.1, f32[1,16]{1,0:T(1,128)} %copy-done.3), custom_call_target="tpu_custom_call" | custom-call | tf_op jit(solution)/shard_map/move_out/pallas_call | solution.py:544
Async XLA Ops:
  112.1 1.7 %copy-start = (f32[128,6144]{1,0:T(8,128)}, f32[128,6144]{1,0:T(8,128)S(1)}, u32[]{:S(2)}) copy-start(f32[128,6144]{1,0:T(8,128)S(1)} %get-tuple-element.13.refs_1_) | copy-start | bytes 9437188
  113.8 1.3 %copy-start.1 = (f32[256,2048]{1,0:T(8,128)}, f32[256,2048]{1,0:T(8,128)S(1)}, u32[]{:S(2)}) copy-start(f32[256,2048]{1,0:T(8,128)S(1)} %get-tuple-element.14.refs_2_) | copy-start | bytes 6291460
  115.1 1.0 copy-start.2
  116.1 0.6 copy-start.3

commit v3 on v2

--- a/solution.py
+++ b/solution.py
@@ -23,10 +23,6 @@
 BF16 = jnp.bfloat16
 F32 = jnp.float32
 
-OFFSETS = (
-    (0, 1), (1, 0), (0, -1), (-1, 0), (1, 1), (-1, -1), (1, -1), (-1, 1),
-    (0, 2), (2, 0), (1, 2), (2, 1), (-1, 2), (2, -1), (2, 2),
-)
 POS, WEIGHT, BUCKET, REF, EMB, MIX = 0, 1, 2, 3, 4, 6
 KEY, QUERY, VALUE, AIM = 0, 1, 2, 3
 SLOT = {AIM: KEY, VALUE: QUERY, QUERY: VALUE, KEY: AIM}
@@ -60,12 +56,15 @@
 
     side = 1 - 2 * lax.rem(sample, 2)
 
-    def peer(step):
-        return lax.rem(my_z + side * step[0] + 4, 4) * 4 + lax.rem(my_y + side * step[1] + 4, 4)
+    def shard_at(slot):
+        along, shift = lax.rem(slot, 4), slot // 4
+        return lax.rem(my_z + 4 + side * along, 4) * 4 + lax.rem(my_y + 8 + side * (along + shift), 4)
+
+    peers = [shard_at(slot) for slot in range(1, shards)]
 
     barrier = pltpu.get_barrier_semaphore()
-    for step in OFFSETS:
-        pl.semaphore_signal(barrier, inc=1, device_id={"seq": peer(step)}, device_id_type=MESH)
+    for peer in peers:
+        pl.semaphore_signal(barrier, inc=1, device_id={"seq": peer}, device_id_type=MESH)
     for turn in range(1, copies):
         other = lax.rem(sample + turn, copies)
         pl.semaphore_signal(barrier, inc=1, device_id={"dp": other}, device_id_type=MESH)
@@ -89,10 +88,10 @@
     pl.semaphore_wait(barrier, shards - 1 + copies - 1)
 
     meta_all[me] = meta[...]
-    for step in OFFSETS:
+    for peer in peers:
         pltpu.make_async_remote_copy(
             meta, meta_all.at[me], small_send.at[0], small_recv.at[0],
-            device_id={"seq": peer(step)}, device_id_type=MESH,
+            device_id={"seq": peer}, device_id_type=MESH,
         ).start()
     mod_copy = pltpu.make_async_copy(
         mod_w.at[:, pl.ds(pl.multiple_of(me * DIM, DIM), DIM)], mod_buf, mod_sem
@@ -108,11 +107,10 @@
 
     def send(part):
         pltpu.make_async_copy(source(part, me), landing(part), recv_sem.at[part]).start()
-        for step in OFFSETS:
-            head = peer(step)
+        for peer in peers:
             pltpu.make_async_remote_copy(
-                source(part, head), landing(part), send_sem.at[part], recv_sem.at[part],
-                device_id={"seq": head}, device_id_type=MESH,
+                source(part, peer), landing(part), send_sem.at[part], recv_sem.at[part],
+                device_id={"seq": peer}, device_id_type=MESH,
             ).start()
 
     def wait_sent(part):
@@ -140,7 +138,8 @@
 
     def perm_block(block, carry):
         at = pl.multiple_of(block * 256, 256)
-        place = (lax.broadcasted_iota(jnp.int32, (256, DIM), 0) + at).astype(F32)
+        inside = lax.broadcasted_iota(jnp.int32, (DIM, DIM), 0)
+        place = jnp.concatenate([inside + shard_at(2 * block + half) * DIM for half in range(2)], axis=0).astype(F32)
         for shard in range(shards):
             hit = place == meta_all[shard, POS : POS + 1, :]
             perm[pl.ds(at, 256), shard * DIM : (shard + 1) * DIM] = jnp.where(hit, 1.0, 0.0).astype(BF16)
@@ -240,8 +239,9 @@
         base = att_out if part == AIM else grad_out
         return base.at[:, pl.ds(pl.multiple_of(PART_COLUMN[part] + me * DIM, DIM), DIM)]
 
-    def give(part, shard):
-        block = got.at[SLOT[part], pl.ds(pl.multiple_of(shard * DIM, DIM), DIM), :]
+    def give(part, slot):
+        block = got.at[SLOT[part], pl.ds(pl.multiple_of(slot * DIM, DIM), DIM), :]
+        shard = shard_at(slot)
 
         @pl.when(shard != me)
         def _():
@@ -254,20 +254,14 @@
         def _():
             pltpu.make_async_copy(block, target(part), back_recv.at[part]).start()
 
-    def pair_of(turn):
-        return lax.rem(my_z + 6 + side * (turn // 2), 4) * 2 + lax.rem(my_y // 2 + 1 + lax.rem(turn, 2), 2)
-
-    def row_of(turn):
-        return lax.rem(my_z + 6 + side * turn, 4)
-
     reorder(VALUE, 1.0, v3, vt)
 
     def output_block(turn, buffer):
-        at = pl.multiple_of(pair_of(turn) * 256, 256)
+        at = pl.multiple_of(turn * 256, 256)
         buffer[0:DIM, :] = by_columns(vt, e_hi[:, pl.ds(at, 256)], e_lo[:, pl.ds(at, 256)])
 
     def attended_block(turn, buffer):
-        at = pl.multiple_of(pair_of(turn) * 256, 256)
+        at = pl.multiple_of(turn * 256, 256)
         out = buffer[0:DIM, :] * inv_sum[0:1, pl.ds(at, 256)]
         head_out[:, pl.ds(at, 256)] = out
         for half in range(2):
@@ -277,7 +271,7 @@
     def give_pair(part):
         def finish(turn):
             for half in range(2):
-                give(part, pair_of(turn) * 2 + half)
+                give(part, turn * 2 + half)
 
         return finish
 
@@ -297,12 +291,12 @@
         aim = placed[:, :DIM] + placed[:, DIM:]
         total = jnp.zeros((DIM, DIM), F32)
         for quarter in range(4):
-            shard = block * 4 + quarter
+            slot = block * 4 + quarter
             begin = pl.multiple_of(at + quarter * DIM, DIM)
             out = head_out[:, pl.ds(begin, DIM)]
             gap = gain * out - aim[quarter * DIM : (quarter + 1) * DIM, :].T
-            loss_rows[shard] = jnp.broadcast_to(jnp.sum(gap * gap, axis=0, keepdims=True), (8, DIM))
-            up_a = gap * meta_all[shard, WEIGHT : WEIGHT + 1, :]
+            loss_rows[slot] = jnp.broadcast_to(jnp.sum(gap * gap, axis=0, keepdims=True), (8, DIM))
+            up_a = gap * meta_all[shard_at(slot), WEIGHT : WEIGHT + 1, :]
             total = total + up_a * out
             up = gain * up_a * inv_sum[0:1, pl.ds(begin, DIM)]
             delta[:, pl.ds(begin, DIM)] = jnp.broadcast_to(jnp.sum(up * out, axis=0, keepdims=True), (8, DIM))
@@ -316,18 +310,17 @@
 
     gain_grad = jnp.sum(gain_sum[...].T, axis=0, keepdims=True)
     row_index = lax.broadcasted_iota(jnp.int32, (8, DIM), 0)
-    for shard in range(shards):
-        tile1[shard] = jnp.where(row_index == 0, loss_rows[shard], jnp.broadcast_to(gain_grad, (8, DIM)))
-    stage1[me] = tile1[me]
-    for step in OFFSETS:
-        shard = peer(step)
+    for slot in range(shards):
+        tile1[slot] = jnp.where(row_index == 0, loss_rows[slot], jnp.broadcast_to(gain_grad, (8, DIM)))
+    stage1[me] = tile1[0]
+    for slot, peer in enumerate(peers):
         pltpu.make_async_remote_copy(
-            tile1.at[shard], stage1.at[me], small_send.at[1], small_recv.at[1],
-            device_id={"seq": shard}, device_id_type=MESH,
+            tile1.at[slot + 1], stage1.at[me], small_send.at[1], small_recv.at[1],
+            device_id={"seq": peer}, device_id_type=MESH,
         ).start()
 
     def value_grad_block(turn, carry):
-        block = row_of(turn)
+        block = turn
         at = pl.multiple_of(block * 512, 512)
         got[SLOT[VALUE], pl.ds(at, 512), :] = by_rows(at, u3.at[:, DIM : 3 * DIM])
         for quarter in range(4):
@@ -339,11 +332,11 @@
     hi_a, lo_a, hi_b, lo_b = (perm.at[:, at : at + 256] for at in range(0, 1024, 256))
 
     def prob_grad_block(turn, buffer):
-        at = pl.multiple_of(pair_of(turn) * 256, 256)
+        at = pl.multiple_of(turn * 256, 256)
         buffer[...] = dot_nt(v3[...], u3[pl.ds(at, 256), :])
 
     def score_grad_block(turn, buffer, high, low):
-        at = pl.multiple_of(pair_of(turn) * 256, 256)
+        at = pl.multiple_of(turn * 256, 256)
         shift = delta[0:1, pl.ds(at, 256)]
         for row in range(0, length, CHUNK):
             here = (slice(row, row + CHUNK), pl.ds(at, 256))
@@ -355,7 +348,7 @@
             e_lo[here] = lo
 
     def query_grad_block(turn, high, low):
-        at = pl.multiple_of(pair_of(turn) * 256, 256)
+        at = pl.multiple_of(turn * 256, 256)
         grad = by_columns(kt, high[...], low[...]) * SCALE
         for half in range(2):
             begin = pl.multiple_of(at + half * DIM, DIM)
@@ -409,7 +402,7 @@
         ).start()
 
     def key_grad_block(turn, carry):
-        block = row_of(turn)
+        block = turn
         at = pl.multiple_of(block * 512, 512)
         got[SLOT[KEY], pl.ds(at, 512), :] = by_rows(at, q3.at[:, DIM : 3 * DIM]) * (1.0 / LOG2E)
         for quarter in range(4):
@@ -425,10 +418,10 @@
         sums = sums + stage2[other, shards : shards + 8, :]
     tile3[...] = sums
     stage3[me] = sums
-    for step in OFFSETS:
+    for peer in peers:
         pltpu.make_async_remote_copy(
             tile3, stage3.at[me], small_send.at[3], small_recv.at[3],
-            device_id={"seq": peer(step)}, device_id_type=MESH,
+            device_id={"seq": peer}, device_id_type=MESH,
         ).start()
 
     by_sample = jnp.concatenate(
@@ -547,8 +540,9 @@
         in_specs=[vmem_spec] * 4,
         out_specs=(any_spec,) * 4,
         scratch_shapes=[dma((13,))],
+        compiler_params=pltpu.CompilerParams(vmem_limit_bytes=1024 * 1024),
         name="move_out",
-    )(*results)
+    )(*(pltpu.with_memory_space_constraint(item, pltpu.VMEM) for item in results))
     return attended[None], grads[None], weight_grad, mixture[0]
 
 

time: 123 us -> 109 us (0.89)
  Pallas kernels: 116 us -> 107 us
  local copies, waits for them, and re-layouts: 4.56 us -> 0 us
    pallas_call x1, Pallas kernels: 111 us -> 104 us  [body(): pl.pallas_call(functools.partial(kernel, shards, copies), out_shape=(pltp...]
    unnamed x8 -> x0, local copies, waits for them, and re-layouts: 4.56 us -> none
    pallas_call x1, Pallas kernels: 5.62 us -> 2.76 us  [body(): pl.pallas_call(move_out, out_shape=tuple((jax.ShapeDtypeStruct(item.shape...]
where the time goes in v3:
time: 109 us; the launch traced here: 108 us
  Pallas kernels  107 us (98%)
  between operations  1.47 us (1%)
    pallas_call x1, Pallas kernels, body(): pl.pallas_call(functools.partial(kernel, shards, copies), out_shape=(pltp...  104 us
    pallas_call x1, Pallas kernels, body(): pl.pallas_call(move_out, out_shape=tuple((jax.ShapeDtypeStruct(item.shape...  2.76 us

profile of v3, /device:TPU:1, one launch (start us, length us, event | category | flops | bytes accessed | tf_op | source)
XLA Modules:
  0.0 108.4 jit_solution(8801387283290913208)
XLA Ops:
  1.3 104.1 %attend.1 = (f32[128,2048]{1,0:T(8,128)S(1)}, f32[128,6144]{1,0:T(8,128)S(1)}, f32[256,2048]{1,0:T(8,128)S(1)}, f32[1,16]{1,0:T(1,128)S(1)}) custom-call(f32[128,6144]{1,0:T(8,128)} %bitcast.5, f32[128,2048]{1,0:T(8,128)} %bitcast.6, s32[1,128]{1,0:T(1,128)} %places.1, s32[1,128]{1,0:T(1,128)} %buckets.1, f32[1,128]{1,0:T(1,128)} %ref_row.1, ...), custom_call_target="tpu_custom_call" | custom-call | tf_op jit(solution)/shard_map/attend/pallas_call | solution.py:491
  105.4 2.8 %move_out.1 = (f32[128,2048]{1,0:T(8,128)}, f32[128,6144]{1,0:T(8,128)}, f32[256,2048]{1,0:T(8,128)}, f32[1,16]{1,0:T(1,128)}) custom-call(f32[128,2048]{1,0:T(8,128)S(1)} %get-tuple-element.12.refs_0_, f32[128,6144]{1,0:T(8,128)S(1)} %get-tuple-element.13.refs_1_, f32[256,2048]{1,0:T(8,128)S(1)} %get-tuple-element.14.refs_2_, ...), custom_call_target="tpu_custom_call" | custom-call | tf_op jit(solution)/shard_map/move_out/pallas_call | solution.py:537

commit v4 on v3

--- a/solution.py
+++ b/solution.py
@@ -43,11 +43,11 @@
 
 
 def kernel(
-    shards, copies, rows, aims, places, buckets, ref_row, steps, old, frequency, mod_w,
+    shards, copies, rows, aims, places_in, buckets_in, ref_in, steps_in, old_in, frequency_in, mod_w,
     att_out, grad_out, weight_out, mix_out,
-    meta, meta_all, got, mod_buf, perm, cat, k3, kt, q3, v3, vt, u3, e_hi, e_lo, head_out, inv_sum, delta,
+    places, buckets, ref_row, frequency, steps, old, meta, meta_all, got, mod_buf, perm, cat, k3, kt, q3, v3, vt, u3, e_hi, e_lo, head_out, inv_sum, delta,
     gain_sum, score_a, score_b, loss_rows, stage1, tile1, stage2, tile2, stage3, tile3,
-    send_sem, recv_sem, back_send, back_recv, small_send, small_recv, mod_sem,
+    send_sem, recv_sem, back_send, back_recv, small_send, small_recv, mod_sem, operand_sem,
 ):
     length = shards * DIM
     me = lax.axis_index("seq")
@@ -69,6 +69,46 @@
         other = lax.rem(sample + turn, copies)
         pl.semaphore_signal(barrier, inc=1, device_id={"dp": other}, device_id_type=MESH)
 
+    operands = [
+        pltpu.make_async_copy(source, into, operand_sem.at[index])
+        for index, (source, into) in enumerate(
+            (
+                (places_in, places), (buckets_in, buckets), (ref_in, ref_row), (frequency_in, frequency),
+                (steps_in, steps), (old_in, old),
+            )
+        )
+    ]
+    for operand in operands:
+        operand.start()
+    mod_copy = pltpu.make_async_copy(
+        mod_w.at[:, pl.ds(pl.multiple_of(me * DIM, DIM), DIM)], mod_buf, mod_sem
+    )
+    mod_copy.start()
+    pl.semaphore_wait(barrier, shards - 1 + copies - 1)
+
+    def source(part, head):
+        base = aims if part == AIM else rows
+        return base.at[:, pl.ds(pl.multiple_of(PART_COLUMN[part] + head * DIM, DIM), DIM)]
+
+    def landing(part):
+        return got.at[part, pl.ds(pl.multiple_of(me * DIM, DIM), DIM), :]
+
+    def send(part):
+        pltpu.make_async_copy(source(part, me), landing(part), recv_sem.at[part]).start()
+        for peer in peers:
+            pltpu.make_async_remote_copy(
+                source(part, peer), landing(part), send_sem.at[part], recv_sem.at[part],
+                device_id={"seq": peer}, device_id_type=MESH,
+            ).start()
+
+    def wait_sent(part):
+        sent = got.at[part, pl.ds(0, (shards - 1) * DIM), :]
+        pltpu.make_async_copy(sent, sent, send_sem.at[part]).wait()
+
+    send(KEY)
+
+    for operand in operands:
+        operand.wait()
     meta[POS : POS + 1, :] = places[...].astype(F32)
     bucket_row = buckets[...]
     lane = lax.broadcasted_iota(jnp.int32, (1, DIM), 1)
@@ -85,46 +125,17 @@
         meta[row : row + 1, :] = wave / (1.0 + jnp.exp(-wave))
     meta[MIX : MIX + 1, :] = old_row
     meta[MIX + 1 : MIX + 2, :] = jnp.zeros((1, DIM), F32)
-    pl.semaphore_wait(barrier, shards - 1 + copies - 1)
-
     meta_all[me] = meta[...]
     for peer in peers:
         pltpu.make_async_remote_copy(
-            meta, meta_all.at[me], small_send.at[0], small_recv.at[0],
+            meta.at[pl.ds(0, 2)], meta_all.at[me, pl.ds(0, 2)], small_send.at[0], small_recv.at[0],
             device_id={"seq": peer}, device_id_type=MESH,
         ).start()
-    mod_copy = pltpu.make_async_copy(
-        mod_w.at[:, pl.ds(pl.multiple_of(me * DIM, DIM), DIM)], mod_buf, mod_sem
-    )
-    mod_copy.start()
-
-    def source(part, head):
-        base = aims if part == AIM else rows
-        return base.at[:, pl.ds(pl.multiple_of(PART_COLUMN[part] + head * DIM, DIM), DIM)]
-
-    def landing(part):
-        return got.at[part, pl.ds(pl.multiple_of(me * DIM, DIM), DIM), :]
-
-    def send(part):
-        pltpu.make_async_copy(source(part, me), landing(part), recv_sem.at[part]).start()
-        for peer in peers:
-            pltpu.make_async_remote_copy(
-                source(part, peer), landing(part), send_sem.at[part], recv_sem.at[part],
-                device_id={"seq": peer}, device_id_type=MESH,
-            ).start()
-
-    def wait_sent(part):
-        sent = got.at[part, pl.ds(0, (shards - 1) * DIM), :]
-        pltpu.make_async_copy(sent, sent, send_sem.at[part]).wait()
-
-    send(KEY)
     send(QUERY)
 
-    def wait_small(stage, buffer, count):
-        pltpu.make_async_copy(buffer.at[pl.ds(0, count)], buffer.at[pl.ds(0, count)], small_recv.at[stage]).wait()
-
-    def wait_small_send(stage, buffer, count):
-        pltpu.make_async_copy(buffer.at[pl.ds(0, count)], buffer.at[pl.ds(0, count)], small_send.at[stage]).wait()
+    def wait_small(sem, buffer, count, depth=2):
+        taken = buffer.at[pl.ds(0, count), pl.ds(0, depth)]
+        pltpu.make_async_copy(taken, taken, sem).wait()
 
     mod_copy.wait()
     embedding = jnp.concatenate([meta[EMB : EMB + 1, :], meta[EMB + 1 : EMB + 2, :]], axis=1)
@@ -134,7 +145,7 @@
     )
     gain = jnp.broadcast_to(gain_row[0:1, :], (DIM, DIM)).T
 
-    wait_small(0, meta_all, shards - 1)
+    wait_small(small_recv.at[0], meta_all, shards - 1)
 
     def perm_block(block, carry):
         at = pl.multiple_of(block * 256, 256)
@@ -315,7 +326,7 @@
     stage1[me] = tile1[0]
     for slot, peer in enumerate(peers):
         pltpu.make_async_remote_copy(
-            tile1.at[slot + 1], stage1.at[me], small_send.at[1], small_recv.at[1],
+            tile1.at[slot + 1, pl.ds(0, 2)], stage1.at[me, pl.ds(0, 2)], small_send.at[1], small_recv.at[1],
             device_id={"seq": peer}, device_id_type=MESH,
         ).start()
 
@@ -328,6 +339,29 @@
         return carry
 
     lax.fori_loop(0, shards // 4, value_grad_block, 0)
+
+    def exchange_losses():
+        wait_small(small_recv.at[1], stage1, shards - 1)
+        loss = jnp.zeros((1, DIM), F32)
+        for shard in range(shards):
+            loss = loss + stage1[shard, 0:1, :]
+        excess = jnp.maximum(0.5 * loss / WIDTH - meta[REF : REF + 1, :], 0.0)
+        hit = lax.broadcasted_iota(jnp.int32, (DIM, DIM), 0).astype(F32) == meta[BUCKET : BUCKET + 1, :]
+        sums = lax.dot_general(
+            jnp.where(row_index == 0, jnp.broadcast_to(excess, (8, DIM)), 1.0), jnp.where(hit, 1.0, 0.0),
+            (((1,), (1,)), ((), ())), precision=HIGHEST, preferred_element_type=F32,
+        )
+        for shard in range(shards):
+            tile2[shard : shard + 1, :] = stage1[shard, 1:2, :]
+        tile2[shards : shards + 2, :] = sums[0:2, :]
+        tile2[shards + 2 : shards + 4, :] = meta[EMB : EMB + 2, :]
+        stage2[sample] = tile2[...]
+        for turn in range(1, copies):
+            other = lax.rem(sample + turn, copies)
+            pltpu.make_async_remote_copy(
+                tile2.at[pl.ds(0, shards + 4)], stage2.at[sample, pl.ds(0, shards + 4)], small_send.at[2], small_recv.at[2],
+                device_id={"dp": other}, device_id_type=MESH,
+            ).start()
 
     hi_a, lo_a, hi_b, lo_b = (perm.at[:, at : at + 256] for at in range(0, 1024, 256))
 
@@ -369,6 +403,7 @@
         query_grad_block(turn, hi_b, lo_b)
         give_queries(turn - 1)
         give_queries(turn)
+        pl.when(pair == 1)(exchange_losses)
         return carry
 
     last = shards // 2 - 1
@@ -379,27 +414,19 @@
     give_queries(last - 1)
     give_queries(last)
 
-    wait_small(1, stage1, shards - 1)
-    loss = jnp.zeros((1, DIM), F32)
-    for shard in range(shards):
-        loss = loss + stage1[shard, 0:1, :]
-    excess = jnp.maximum(0.5 * loss / WIDTH - meta[REF : REF + 1, :], 0.0)
-    hit = lax.broadcasted_iota(jnp.int32, (DIM, DIM), 0).astype(F32) == meta[BUCKET : BUCKET + 1, :]
-    sums = lax.dot_general(
-        jnp.where(row_index == 0, jnp.broadcast_to(excess, (8, DIM)), 1.0), jnp.where(hit, 1.0, 0.0),
-        (((1,), (1,)), ((), ())), precision=HIGHEST, preferred_element_type=F32,
-    )
-    for shard in range(shards):
-        tile2[shard : shard + 1, :] = stage1[shard, 1:2, :]
-    tile2[shards : shards + 8, :] = sums
-    tile2[shards + 2 : shards + 4, :] = meta[EMB : EMB + 2, :]
-    stage2[sample] = tile2[...]
-    for turn in range(1, copies):
-        other = lax.rem(sample + turn, copies)
-        pltpu.make_async_remote_copy(
-            tile2, stage2.at[sample], small_send.at[2], small_recv.at[2],
-            device_id={"dp": other}, device_id_type=MESH,
-        ).start()
+    def exchange_sums():
+        if copies > 1:
+            wait_small(small_recv.at[2], stage2, copies - 1, shards + 4)
+        sums = jnp.zeros((2, DIM), F32)
+        for other in range(copies):
+            sums = sums + stage2[other, shards : shards + 2, :]
+        tile3[0:2, :] = sums
+        stage3[me, 0:2, :] = sums
+        for peer in peers:
+            pltpu.make_async_remote_copy(
+                tile3.at[pl.ds(0, 2)], stage3.at[me, pl.ds(0, 2)], small_send.at[3], small_recv.at[3],
+                device_id={"seq": peer}, device_id_type=MESH,
+            ).start()
 
     def key_grad_block(turn, carry):
         block = turn
@@ -407,22 +434,10 @@
         got[SLOT[KEY], pl.ds(at, 512), :] = by_rows(at, q3.at[:, DIM : 3 * DIM]) * (1.0 / LOG2E)
         for quarter in range(4):
             give(KEY, block * 4 + quarter)
+        pl.when(turn == 1)(exchange_sums)
         return carry
 
     lax.fori_loop(0, shards // 4, key_grad_block, 0)
-
-    if copies > 1:
-        wait_small(2, stage2, copies - 1)
-    sums = jnp.zeros((8, DIM), F32)
-    for other in range(copies):
-        sums = sums + stage2[other, shards : shards + 8, :]
-    tile3[...] = sums
-    stage3[me] = sums
-    for peer in peers:
-        pltpu.make_async_remote_copy(
-            tile3, stage3.at[me], small_send.at[3], small_recv.at[3],
-            device_id={"seq": peer}, device_id_type=MESH,
-        ).start()
 
     by_sample = jnp.concatenate(
         [
@@ -437,10 +452,10 @@
         weight_out[:, head * DIM : (head + 1) * DIM] = lax.dot_general(
             by_frequency, gains, (((1,), (0,)), ((), ())), precision=HIGHEST, preferred_element_type=F32
         )
-    wait_small(3, stage3, shards - 1)
-    sums = jnp.zeros((8, DIM), F32)
+    wait_small(small_recv.at[3], stage3, shards - 1)
+    sums = jnp.zeros((2, DIM), F32)
     for shard in range(shards):
-        sums = sums + stage3[shard]
+        sums = sums + stage3[shard, 0:2, :]
     mean = sums[0:1, :] / jnp.maximum(sums[1:2, :], 1.0)
     updated = meta[MIX : MIX + 1, :] * (1.0 + RATE * mean)
     updated = jnp.where(lane < BUCKETS, updated, 0.0)
@@ -456,11 +471,11 @@
         base = att_out if part == AIM else grad_out
         landed = base.at[:, PART_COLUMN[part] : PART_COLUMN[part] + WIDTH]
         pltpu.make_async_copy(landed, landed, back_recv.at[part]).wait()
-    wait_small_send(0, meta_all, shards - 1)
-    wait_small_send(1, stage1, shards - 1)
+    wait_small(small_send.at[0], meta_all, shards - 1)
+    wait_small(small_send.at[1], stage1, shards - 1)
     if copies > 1:
-        wait_small_send(2, stage2, copies - 1)
-    wait_small_send(3, stage3, shards - 1)
+        wait_small(small_send.at[2], stage2, copies - 1, shards + 4)
+    wait_small(small_send.at[3], stage3, shards - 1)
 
 
 def move_out(*refs):
@@ -487,7 +502,6 @@
     any_spec = pl.BlockSpec(memory_space=pl.ANY)
     vmem_spec = pl.BlockSpec(memory_space=pltpu.VMEM)
     dma = pltpu.SemaphoreType.DMA
-    smem_spec = pl.BlockSpec(memory_space=pltpu.SMEM)
     attended, grads, weight_grad, mixture = pl.pallas_call(
         functools.partial(kernel, shards, copies),
         out_shape=(
@@ -496,9 +510,15 @@
             pltpu.VMEM((FREQ_DIM, WIDTH), F32),
             pltpu.VMEM((1, BUCKETS), F32),
         ),
-        in_specs=[any_spec, any_spec, vmem_spec, vmem_spec, vmem_spec, smem_spec, smem_spec, vmem_spec, any_spec],
+        in_specs=[any_spec] * 9,
         out_specs=(vmem_spec, vmem_spec, vmem_spec, vmem_spec),
         scratch_shapes=[
+            pltpu.VMEM((1, DIM), jnp.int32),
+            pltpu.VMEM((1, DIM), jnp.int32),
+            pltpu.VMEM((1, DIM), F32),
+            pltpu.VMEM((1, DIM), F32),
+            pltpu.SMEM((1,), jnp.int32),
+            pltpu.SMEM((BUCKETS,), F32),
             pltpu.VMEM((8, DIM), F32),
             pltpu.VMEM((shards, 8, DIM), F32),
             pltpu.VMEM((4, length, DIM), F32),
@@ -526,7 +546,7 @@
             pltpu.VMEM((shards + 8, DIM), F32),
             pltpu.VMEM((shards, 8, DIM), F32),
             pltpu.VMEM((8, DIM), F32),
-            dma((4,)), dma((4,)), dma((4,)), dma((4,)), dma((4,)), dma((4,)), dma,
+            dma((4,)), dma((4,)), dma((4,)), dma((4,)), dma((4,)), dma((4,)), dma, dma((6,)),
         ],
         compiler_params=pltpu.CompilerParams(
             collective_id=0, has_side_effects=True, vmem_limit_bytes=56 * 1024 * 1024

time: 109 us -> 106 us (0.972)
  Pallas kernels: 107 us -> 104 us
    pallas_call x1, Pallas kernels: 104 us -> 102 us  [body(): pl.pallas_call(functools.partial(kernel, shards, copies), out_shape=(pltp...]
where the time goes in v4:
time: 106 us
  Pallas kernels  104 us (98%)
  between operations  1.47 us (1%)
    pallas_call x1, Pallas kernels, body(): pl.pallas_call(functools.partial(kernel, shards, copies), out_shape=(pltp...  102 us
    pallas_call x1, Pallas kernels, body(): pl.pallas_call(move_out, out_shape=tuple((jax.ShapeDtypeStruct(item.shape...  2.76 us

profile of v4, /device:TPU:1, one launch (start us, length us, event | category | flops | bytes accessed | tf_op | source)
XLA Modules:
  0.0 105.9 jit_solution(5801838979457642530)
XLA Ops:
  1.3 101.7 %attend.1 = (f32[128,2048]{1,0:T(8,128)S(1)}, f32[128,6144]{1,0:T(8,128)S(1)}, f32[256,2048]{1,0:T(8,128)S(1)}, f32[1,16]{1,0:T(1,128)S(1)}) custom-call(f32[128,6144]{1,0:T(8,128)} %bitcast.5, f32[128,2048]{1,0:T(8,128)} %bitcast.6, s32[1,128]{1,0:T(1,128)} %places_in.1, s32[1,128]{1,0:T(1,128)} %buckets_in.1, f32[1,128]{1,0:T(1,128)} %ref_in.1, ...), custom_call_target="tpu_custom_call" | custom-call | tf_op jit(solution)/shard_map/attend/pallas_call | solution.py:505
  103.0 2.8 %move_out.1 = (f32[128,2048]{1,0:T(8,128)}, f32[128,6144]{1,0:T(8,128)}, f32[256,2048]{1,0:T(8,128)}, f32[1,16]{1,0:T(1,128)}) custom-call(f32[128,2048]{1,0:T(8,128)S(1)} %get-tuple-element.12.refs_0_, f32[128,6144]{1,0:T(8,128)S(1)} %get-tuple-element.13.refs_1_, f32[256,2048]{1,0:T(8,128)S(1)} %get-tuple-element.14.refs_2_, ...), custom_call_target="tpu_custom_call" | custom-call | tf_op jit(solution)/shard_map/move_out/pallas_call | solution.py:557

commit v5 on v4

--- a/solution.py
+++ b/solution.py
@@ -15,7 +15,8 @@
 BUCKETS = 16
 WIDTH = HEADS * DIM
 RATE = 10.0
-CHUNK = 64
+COLS = 512
+CHUNK = 32
 LOG2E = 1.4426950408889634
 SCALE = DIM ** (-0.5)
 MESH = pl.DeviceIdType.MESH
@@ -194,11 +195,11 @@
 
         def make(block, buffer):
             at = pl.multiple_of(block * 512, 512)
-            buffer[0:512, :] = dot(perm[pl.ds(at, 512), :], cat[...])
+            buffer[0:512, 0:256] = dot(perm[pl.ds(at, 512), :], cat[...])
 
         def use(block, buffer):
             at = pl.multiple_of(block * 512, 512)
-            placed = buffer[0:512, :]
+            placed = buffer[0:512, 0:256]
             hi, lo = placed[:, :DIM].astype(BF16), placed[:, DIM:].astype(BF16)
             into[pl.ds(at, 512), 0:DIM] = hi
             into[pl.ds(at, 512), DIM : 2 * DIM] = hi if part == QUERY else lo
@@ -226,25 +227,25 @@
     reorder(QUERY, SCALE * LOG2E, q3, None)
 
     def score_block(block, buffer):
-        at = pl.multiple_of(block * 256, 256)
-        buffer[...] = dot_nt(k3[...], q3[pl.ds(at, 256), :])
+        at = pl.multiple_of(block * COLS, COLS)
+        buffer[...] = dot_nt(k3[...], q3[pl.ds(at, COLS), :])
 
     def softmax_block(block, buffer):
-        at = pl.multiple_of(block * 256, 256)
-        top = jnp.full((8, 256), -jnp.inf, F32)
+        at = pl.multiple_of(block * COLS, COLS)
+        top = jnp.full((8, COLS), -jnp.inf, F32)
         for row in range(0, length, CHUNK):
-            top = jnp.maximum(top, jnp.max(buffer[row : row + CHUNK, :].reshape(CHUNK // 8, 8, 256), axis=0))
+            top = jnp.maximum(top, jnp.max(buffer[row : row + CHUNK, :].reshape(CHUNK // 8, 8, COLS), axis=0))
         top = jnp.max(top, axis=0, keepdims=True)
-        sums = jnp.zeros((8, 256), F32)
+        sums = jnp.zeros((8, COLS), F32)
         for row in range(0, length, CHUNK):
             weights = jnp.exp2(buffer[row : row + CHUNK, :] - top)
-            sums = sums + jnp.sum(weights.reshape(CHUNK // 8, 8, 256), axis=0)
+            sums = sums + jnp.sum(weights.reshape(CHUNK // 8, 8, COLS), axis=0)
             hi, lo = split(weights)
-            e_hi[row : row + CHUNK, pl.ds(at, 256)] = hi
-            e_lo[row : row + CHUNK, pl.ds(at, 256)] = lo
-        inv_sum[:, pl.ds(at, 256)] = jnp.broadcast_to(1.0 / jnp.sum(sums, axis=0, keepdims=True), (8, 256))
-
-    pipeline(length // 256, score_block, softmax_block)
+            e_hi[row : row + CHUNK, pl.ds(at, COLS)] = hi
+            e_lo[row : row + CHUNK, pl.ds(at, COLS)] = lo
+        inv_sum[:, pl.ds(at, COLS)] = jnp.broadcast_to(1.0 / jnp.sum(sums, axis=0, keepdims=True), (8, COLS))
+
+    pipeline(length // COLS, score_block, softmax_block)
 
     def target(part):
         base = att_out if part == AIM else grad_out
@@ -268,37 +269,37 @@
     reorder(VALUE, 1.0, v3, vt)
 
     def output_block(turn, buffer):
-        at = pl.multiple_of(turn * 256, 256)
-        buffer[0:DIM, :] = by_columns(vt, e_hi[:, pl.ds(at, 256)], e_lo[:, pl.ds(at, 256)])
+        at = pl.multiple_of(turn * COLS, COLS)
+        buffer[0:DIM, :] = by_columns(vt, e_hi[:, pl.ds(at, COLS)], e_lo[:, pl.ds(at, COLS)])
 
     def attended_block(turn, buffer):
-        at = pl.multiple_of(turn * 256, 256)
-        out = buffer[0:DIM, :] * inv_sum[0:1, pl.ds(at, 256)]
-        head_out[:, pl.ds(at, 256)] = out
-        for half in range(2):
+        at = pl.multiple_of(turn * COLS, COLS)
+        out = buffer[0:DIM, :] * inv_sum[0:1, pl.ds(at, COLS)]
+        head_out[:, pl.ds(at, COLS)] = out
+        for half in range(COLS // DIM):
             begin = pl.multiple_of(at + half * DIM, DIM)
             got[SLOT[AIM], pl.ds(begin, DIM), :] = (gain * out[:, half * DIM : (half + 1) * DIM]).T
 
     def give_pair(part):
         def finish(turn):
-            for half in range(2):
-                give(part, turn * 2 + half)
+            for half in range(COLS // DIM):
+                give(part, turn * (COLS // DIM) + half)
 
         return finish
 
-    pipeline(shards // 2, output_block, attended_block, give_pair(AIM))
+    pipeline(length // COLS, output_block, attended_block, give_pair(AIM))
 
     arrive(AIM, 1.0)
 
     def aim_block(block, buffer):
         at = pl.multiple_of(block * 512, 512)
-        buffer[0:512, :] = dot(perm[pl.ds(at, 512), :], cat[...])
+        buffer[0:512, 0:256] = dot(perm[pl.ds(at, 512), :], cat[...])
 
     gain_sum[...] = jnp.zeros((DIM, DIM), F32)
 
     def upstream_block(block, buffer):
         at = pl.multiple_of(block * 512, 512)
-        placed = buffer[0:512, :]
+        placed = buffer[0:512, 0:256]
         aim = placed[:, :DIM] + placed[:, DIM:]
         total = jnp.zeros((DIM, DIM), F32)
         for quarter in range(4):
@@ -363,17 +364,17 @@
                 device_id={"dp": other}, device_id_type=MESH,
             ).start()
 
-    hi_a, lo_a, hi_b, lo_b = (perm.at[:, at : at + 256] for at in range(0, 1024, 256))
+    hi_a, lo_a, hi_b, lo_b = (perm.at[:, at : at + COLS] for at in range(0, 4 * COLS, COLS))
 
     def prob_grad_block(turn, buffer):
-        at = pl.multiple_of(turn * 256, 256)
-        buffer[...] = dot_nt(v3[...], u3[pl.ds(at, 256), :])
+        at = pl.multiple_of(turn * COLS, COLS)
+        buffer[...] = dot_nt(v3[...], u3[pl.ds(at, COLS), :])
 
     def score_grad_block(turn, buffer, high, low):
-        at = pl.multiple_of(turn * 256, 256)
-        shift = delta[0:1, pl.ds(at, 256)]
+        at = pl.multiple_of(turn * COLS, COLS)
+        shift = delta[0:1, pl.ds(at, COLS)]
         for row in range(0, length, CHUNK):
-            here = (slice(row, row + CHUNK), pl.ds(at, 256))
+            here = (slice(row, row + CHUNK), pl.ds(at, COLS))
             weights = e_hi[here].astype(F32) + e_lo[here].astype(F32)
             hi, lo = split((buffer[row : row + CHUNK, :] - shift) * weights)
             high[row : row + CHUNK, :] = hi
@@ -382,9 +383,9 @@
             e_lo[here] = lo
 
     def query_grad_block(turn, high, low):
-        at = pl.multiple_of(turn * 256, 256)
+        at = pl.multiple_of(turn * COLS, COLS)
         grad = by_columns(kt, high[...], low[...]) * SCALE
-        for half in range(2):
+        for half in range(COLS // DIM):
             begin = pl.multiple_of(at + half * DIM, DIM)
             got[SLOT[QUERY], pl.ds(begin, DIM), :] = grad[:, half * DIM : (half + 1) * DIM].T
 
@@ -403,10 +404,10 @@
         query_grad_block(turn, hi_b, lo_b)
         give_queries(turn - 1)
         give_queries(turn)
-        pl.when(pair == 1)(exchange_losses)
+        pl.when(pair == last // 2 - 1)(exchange_losses)
         return carry
 
-    last = shards // 2 - 1
+    last = length // COLS - 1
     lax.fori_loop(0, last // 2, gradient_pair, 0)
     score_grad_block(last, score_b, hi_b, lo_b)
     query_grad_block(last - 1, hi_a, lo_a)
@@ -537,8 +538,8 @@
             pltpu.VMEM((8, length), F32),
             pltpu.VMEM((8, length), F32),
             pltpu.VMEM((DIM, DIM), F32),
-            pltpu.VMEM((length, 256), F32),
-            pltpu.VMEM((length, 256), F32),
+            pltpu.VMEM((length, COLS), F32),
+            pltpu.VMEM((length, COLS), F32),
             pltpu.VMEM((shards, 8, DIM), F32),
             pltpu.VMEM((shards, 8, DIM), F32),
             pltpu.VMEM((shards, 8, DIM), F32),

time: 106 us -> 107 us (level)
  no operation moved by 1% of the time
where the time goes in v5:
time: 107 us
  Pallas kernels  105 us (98%)
  between operations  1.47 us (1%)
    pallas_call x1, Pallas kernels, body(): pl.pallas_call(functools.partial(kernel, shards, copies), out_shape=(pltp...  102 us
    pallas_call x1, Pallas kernels, body(): pl.pallas_call(move_out, out_shape=tuple((jax.ShapeDtypeStruct(item.shape...  2.76 us

profile of v5, /device:TPU:1, one launch (start us, length us, event | category | flops | bytes accessed | tf_op | source)
XLA Modules:
  0.0 106.6 jit_solution(4251950535298835057)
XLA Ops:
  1.3 102.3 %attend.1 = (f32[128,2048]{1,0:T(8,128)S(1)}, f32[128,6144]{1,0:T(8,128)S(1)}, f32[256,2048]{1,0:T(8,128)S(1)}, f32[1,16]{1,0:T(1,128)S(1)}) custom-call(f32[128,6144]{1,0:T(8,128)} %bitcast.5, f32[128,2048]{1,0:T(8,128)} %bitcast.6, s32[1,128]{1,0:T(1,128)} %places_in.1, s32[1,128]{1,0:T(1,128)} %buckets_in.1, f32[1,128]{1,0:T(1,128)} %ref_in.1, ...), custom_call_target="tpu_custom_call" | custom-call | tf_op jit(solution)/shard_map/attend/pallas_call | solution.py:506
  103.6 2.8 %move_out.1 = (f32[128,2048]{1,0:T(8,128)}, f32[128,6144]{1,0:T(8,128)}, f32[256,2048]{1,0:T(8,128)}, f32[1,16]{1,0:T(1,128)}) custom-call(f32[128,2048]{1,0:T(8,128)S(1)} %get-tuple-element.12.refs_0_, f32[128,6144]{1,0:T(8,128)S(1)} %get-tuple-element.13.refs_1_, f32[256,2048]{1,0:T(8,128)S(1)} %get-tuple-element.14.refs_2_, ...), custom_call_target="tpu_custom_call" | custom-call | tf_op jit(solution)/shard_map/move_out/pallas_call | solution.py:558

commit v6 on v4

--- a/solution.py
+++ b/solution.py
@@ -54,11 +54,13 @@
     sample = lax.axis_index("dp")
     my_z, my_y = me // 4, lax.rem(me, 4)
 
-    side = 1 - 2 * lax.rem(sample, 2)
+    core = lax.rem(sample, 2)
+    side = 1 - 2 * core
 
     def shard_at(slot):
         along, shift = lax.rem(slot, 4), slot // 4
-        return lax.rem(my_z + 4 + side * along, 4) * 4 + lax.rem(my_y + 8 + side * (along + shift), 4)
+        by_z, by_y = along + core * shift, along + (1 - core) * shift
+        return lax.rem(my_z + 8 + side * by_z, 4) * 4 + lax.rem(my_y + 8 + side * by_y, 4)
 
     peers = [shard_at(slot) for slot in range(1, shards)]
 
@@ -483,7 +485,7 @@
     sources, outputs, sems = refs[:count], refs[count : 2 * count], refs[-1]
     moves = []
     for source, output in zip(sources, outputs):
-        pieces = 4 if source.shape[0] >= DIM else 1
+        pieces = 8 if source.shape[0] >= DIM else 1
         rows = source.shape[0] // pieces
         for piece in range(pieces):
             part = pl.ds(piece * rows, rows)
@@ -559,7 +561,7 @@
         out_shape=tuple(jax.ShapeDtypeStruct(item.shape, F32) for item in results),
         in_specs=[vmem_spec] * 4,
         out_specs=(any_spec,) * 4,
-        scratch_shapes=[dma((13,))],
+        scratch_shapes=[dma((25,))],
         compiler_params=pltpu.CompilerParams(vmem_limit_bytes=1024 * 1024),
         name="move_out",
     )(*(pltpu.with_memory_space_constraint(item, pltpu.VMEM) for item in results))

time: 106 us -> 111 us (1.047)
  the two profiles are of different devices: /device:TPU:1 before, /device:TPU:98 now
where the time goes in v6:
time: 111 us
  Pallas kernels  109 us (98%)
  between operations  1.47 us (1%)
    pallas_call x1, Pallas kernels, body(): pl.pallas_call(functools.partial(kernel, shards, copies), out_shape=(pltp...  107 us
    pallas_call x1, Pallas kernels, body(): pl.pallas_call(move_out, out_shape=tuple((jax.ShapeDtypeStruct(item.shape...  2.85 us

profile of v6, /device:TPU:98, one launch (start us, length us, event | category | flops | bytes accessed | tf_op | source)
XLA Modules:
  0.0 110.9 jit_solution(5071022135992646219)
XLA Ops:
  1.3 106.6 %attend.1 = (f32[128,2048]{1,0:T(8,128)S(1)}, f32[128,6144]{1,0:T(8,128)S(1)}, f32[256,2048]{1,0:T(8,128)S(1)}, f32[1,16]{1,0:T(1,128)S(1)}) custom-call(f32[128,6144]{1,0:T(8,128)} %bitcast.5, f32[128,2048]{1,0:T(8,128)} %bitcast.6, s32[1,128]{1,0:T(1,128)} %places_in.1, s32[1,128]{1,0:T(1,128)} %buckets_in.1, f32[1,128]{1,0:T(1,128)} %ref_in.1, ...), custom_call_target="tpu_custom_call" | custom-call | tf_op jit(solution)/shard_map/attend/pallas_call | solution.py:507
  107.8 2.9 %move_out.1 = (f32[128,2048]{1,0:T(8,128)}, f32[128,6144]{1,0:T(8,128)}, f32[256,2048]{1,0:T(8,128)}, f32[1,16]{1,0:T(1,128)}) custom-call(f32[128,2048]{1,0:T(8,128)S(1)} %get-tuple-element.12.refs_0_, f32[128,6144]{1,0:T(8,128)S(1)} %get-tuple-element.13.refs_1_, f32[256,2048]{1,0:T(8,128)S(1)} %get-tuple-element.14.refs_2_, ...), custom_call_target="tpu_custom_call" | custom-call | tf_op jit(solution)/shard_map/move_out/pallas_call | solution.py:559

commit v7 on v4

--- a/solution.py
+++ b/solution.py
@@ -44,7 +44,7 @@
 
 def kernel(
     shards, copies, rows, aims, places_in, buckets_in, ref_in, steps_in, old_in, frequency_in, mod_w,
-    att_out, grad_out, weight_out, mix_out,
+    back_out, weight_out, mix_out,
     places, buckets, ref_row, frequency, steps, old, meta, meta_all, got, mod_buf, perm, cat, k3, kt, q3, v3, vt, u3, e_hi, e_lo, head_out, inv_sum, delta,
     gain_sum, score_a, score_b, loss_rows, stage1, tile1, stage2, tile2, stage3, tile3,
     send_sem, recv_sem, back_send, back_recv, small_send, small_recv, mod_sem, operand_sem,
@@ -247,8 +247,7 @@
     pipeline(length // 256, score_block, softmax_block)
 
     def target(part):
-        base = att_out if part == AIM else grad_out
-        return base.at[:, pl.ds(pl.multiple_of(PART_COLUMN[part] + me * DIM, DIM), DIM)]
+        return back_out.at[part, me]
 
     def give(part, slot):
         block = got.at[SLOT[part], pl.ds(pl.multiple_of(slot * DIM, DIM), DIM), :]
@@ -468,9 +467,7 @@
             wait_sent(part)
         sent = got.at[SLOT[part], pl.ds(0, others), :]
         pltpu.make_async_copy(sent, sent, back_send.at[part]).wait()
-        base = att_out if part == AIM else grad_out
-        landed = base.at[:, PART_COLUMN[part] : PART_COLUMN[part] + WIDTH]
-        pltpu.make_async_copy(landed, landed, back_recv.at[part]).wait()
+        pltpu.make_async_copy(back_out.at[part], back_out.at[part], back_recv.at[part]).wait()
     wait_small(small_send.at[0], meta_all, shards - 1)
     wait_small(small_send.at[1], stage1, shards - 1)
     if copies > 1:
@@ -478,20 +475,22 @@
     wait_small(small_send.at[3], stage3, shards - 1)
 
 
-def move_out(*refs):
-    count = len(refs) // 2
-    sources, outputs, sems = refs[:count], refs[count : 2 * count], refs[-1]
-    moves = []
-    for source, output in zip(sources, outputs):
-        pieces = 4 if source.shape[0] >= DIM else 1
-        rows = source.shape[0] // pieces
-        for piece in range(pieces):
-            part = pl.ds(piece * rows, rows)
-            moves.append(pltpu.make_async_copy(source.at[part], output.at[part], sems.at[len(moves)]))
-    for move in moves:
-        move.start()
-    for move in moves:
-        move.wait()
+def move_out(back, weight, mixture, att_out, grad_out, weight_out, mix_out, sems):
+    for head in range(HEADS):
+        for part in (KEY, QUERY, VALUE, AIM):
+            base = att_out if part == AIM else grad_out
+            columns = pl.ds(PART_COLUMN[part] + head * DIM, DIM)
+            pltpu.make_async_copy(back.at[part, head], base.at[:, columns], sems.at[part]).start()
+    others = [
+        pltpu.make_async_copy(weight, weight_out, sems.at[4]),
+        pltpu.make_async_copy(mixture, mix_out, sems.at[5]),
+    ]
+    for other in others:
+        other.start()
+    for other in others:
+        other.wait()
+    for part in (KEY, QUERY, VALUE, AIM):
+        pltpu.make_async_copy(back.at[part], back.at[part], sems.at[part]).wait()
 
 
 def body(reader_rows, reader_targets, dest_pos, bucket_ids, ref_loss, timesteps, mod_weight, mixture_old):
@@ -502,16 +501,15 @@
     any_spec = pl.BlockSpec(memory_space=pl.ANY)
     vmem_spec = pl.BlockSpec(memory_space=pltpu.VMEM)
     dma = pltpu.SemaphoreType.DMA
-    attended, grads, weight_grad, mixture = pl.pallas_call(
+    results = pl.pallas_call(
         functools.partial(kernel, shards, copies),
         out_shape=(
-            pltpu.VMEM((DIM, WIDTH), F32),
-            pltpu.VMEM((DIM, 3 * WIDTH), F32),
+            pltpu.VMEM((4, HEADS, DIM, DIM), F32),
             pltpu.VMEM((FREQ_DIM, WIDTH), F32),
             pltpu.VMEM((1, BUCKETS), F32),
         ),
         in_specs=[any_spec] * 9,
-        out_specs=(vmem_spec, vmem_spec, vmem_spec, vmem_spec),
+        out_specs=(vmem_spec, vmem_spec, vmem_spec),
         scratch_shapes=[
             pltpu.VMEM((1, DIM), jnp.int32),
             pltpu.VMEM((1, DIM), jnp.int32),
@@ -553,13 +551,15 @@
         ),
         name="attend",
     )(reader_rows[0], reader_targets[0], dest_pos, bucket_ids, ref_loss, timesteps, mixture_old, frequency, mod_weight)
-    results = (attended, grads, weight_grad, mixture)
     attended, grads, weight_grad, mixture = pl.pallas_call(
         move_out,
-        out_shape=tuple(jax.ShapeDtypeStruct(item.shape, F32) for item in results),
-        in_specs=[vmem_spec] * 4,
+        out_shape=tuple(
+            jax.ShapeDtypeStruct(shape, F32)
+            for shape in ((DIM, WIDTH), (DIM, 3 * WIDTH), (FREQ_DIM, WIDTH), (1, BUCKETS))
+        ),
+        in_specs=[vmem_spec] * 3,
         out_specs=(any_spec,) * 4,
-        scratch_shapes=[dma((13,))],
+        scratch_shapes=[dma((6,))],
         compiler_params=pltpu.CompilerParams(vmem_limit_bytes=1024 * 1024),
         name="move_out",
     )(*(pltpu.with_memory_space_constraint(item, pltpu.VMEM) for item in results))

time: 106 us -> 106 us (level)
  no operation moved by 1% of the time
where the time goes in v7:
time: 106 us
  Pallas kernels  104 us (98%)
  between operations  1.47 us (1%)
    pallas_call x1, Pallas kernels, body(): pl.pallas_call(functools.partial(kernel, shards, copies), out_shape=(pltp...  102 us
    pallas_call x1, Pallas kernels, body(): pl.pallas_call(move_out, out_shape=tuple((jax.ShapeDtypeStruct(shape, F32...  2.73 us

profile of v7, /device:TPU:1, one launch (start us, length us, event | category | flops | bytes accessed | tf_op | source)
XLA Modules:
  0.0 105.8 jit_solution(8748222746206620368)
XLA Ops:
  1.3 101.6 %attend.1 = (f32[4,16,128,128]{3,2,1,0:T(8,128)S(1)}, f32[256,2048]{1,0:T(8,128)S(1)}, f32[1,16]{1,0:T(1,128)S(1)}) custom-call(f32[128,6144]{1,0:T(8,128)} %bitcast.5, f32[128,2048]{1,0:T(8,128)} %bitcast.6, s32[1,128]{1,0:T(1,128)} %places_in.1, s32[1,128]{1,0:T(1,128)} %buckets_in.1, f32[1,128]{1,0:T(1,128)} %ref_in.1, s32[1]{0:T(128)S(6)} %copy.13.steps_in, ...), custom_call_target="tpu_custom_call" | custom-call | tf_op jit(solution)/shard_map/attend/pallas_call | solution.py:504
  102.9 2.7 %move_out.1 = (f32[128,2048]{1,0:T(8,128)}, f32[128,6144]{1,0:T(8,128)}, f32[256,2048]{1,0:T(8,128)}, f32[1,16]{1,0:T(1,128)}) custom-call(f32[4,16,128,128]{3,2,1,0:T(8,128)S(1)} %get-tuple-element.11.back, f32[256,2048]{1,0:T(8,128)S(1)} %get-tuple-element.12.weight, f32[1,16]{1,0:T(1,128)S(1)} %get-tuple-element.13.mixture), custom_call_target="tpu_custom_call" | custom-call | tf_op jit(solution)/shard_map/move_out/pallas_call | solution.py:554

commit v8 on v4

--- a/solution.py
+++ b/solution.py
@@ -23,6 +23,16 @@
 BF16 = jnp.bfloat16
 F32 = jnp.float32
 
+STEPS = (
+    (0, 0), (2, 2), (0, 1), (1, 0), (0, 3), (3, 0), (1, 1), (1, 3),
+    (3, 1), (3, 3), (0, 2), (2, 0), (1, 2), (2, 1), (3, 2), (2, 3),
+)
+
+
+def packed(axis, first):
+    return sum(step[axis] * 4**digit for digit, step in enumerate(STEPS[first : first + 8]))
+
+
 POS, WEIGHT, BUCKET, REF, EMB, MIX = 0, 1, 2, 3, 4, 6
 KEY, QUERY, VALUE, AIM = 0, 1, 2, 3
 SLOT = {AIM: KEY, VALUE: QUERY, QUERY: VALUE, KEY: AIM}
@@ -56,9 +66,15 @@
 
     side = 1 - 2 * lax.rem(sample, 2)
 
+    def step_at(axis, slot):
+        if isinstance(slot, int):
+            return STEPS[slot][axis]
+        digits = jnp.where(slot < 8, packed(axis, 0), packed(axis, 8))
+        return lax.shift_right_logical(digits, 2 * lax.rem(slot, 8)) & 3
+
     def shard_at(slot):
-        along, shift = lax.rem(slot, 4), slot // 4
-        return lax.rem(my_z + 4 + side * along, 4) * 4 + lax.rem(my_y + 8 + side * (along + shift), 4)
+        along_z, along_y = step_at(0, slot), step_at(1, slot)
+        return lax.rem(my_z + 4 + side * along_z, 4) * 4 + lax.rem(my_y + 4 + side * along_y, 4)
 
     peers = [shard_at(slot) for slot in range(1, shards)]
 

time: 106 us -> 108 us (1.019)
  Pallas kernels: 104 us -> 106 us
    pallas_call x1, Pallas kernels: 102 us -> 103 us  [body(): pl.pallas_call(functools.partial(kernel, shards, copies), out_shape=(pltp...]
where the time goes in v8:
time: 108 us
  Pallas kernels  106 us (98%)
  between operations  1.47 us (1%)
    pallas_call x1, Pallas kernels, body(): pl.pallas_call(functools.partial(kernel, shards, copies), out_shape=(pltp...  103 us
    pallas_call x1, Pallas kernels, body(): pl.pallas_call(move_out, out_shape=tuple((jax.ShapeDtypeStruct(item.shape...  2.76 us

profile of v8, /device:TPU:1, one launch (start us, length us, event | category | flops | bytes accessed | tf_op | source)
XLA Modules:
  0.0 107.6 jit_solution(17761029191124598365)
XLA Ops:
  1.3 103.4 %attend.1 = (f32[128,2048]{1,0:T(8,128)S(1)}, f32[128,6144]{1,0:T(8,128)S(1)}, f32[256,2048]{1,0:T(8,128)S(1)}, f32[1,16]{1,0:T(1,128)S(1)}) custom-call(f32[128,6144]{1,0:T(8,128)} %bitcast.5, f32[128,2048]{1,0:T(8,128)} %bitcast.6, s32[1,128]{1,0:T(1,128)} %places_in.1, s32[1,128]{1,0:T(1,128)} %buckets_in.1, f32[1,128]{1,0:T(1,128)} %ref_in.1, ...), custom_call_target="tpu_custom_call" | custom-call | tf_op jit(solution)/shard_map/attend/pallas_call | solution.py:521
  104.7 2.8 %move_out.1 = (f32[128,2048]{1,0:T(8,128)}, f32[128,6144]{1,0:T(8,128)}, f32[256,2048]{1,0:T(8,128)}, f32[1,16]{1,0:T(1,128)}) custom-call(f32[128,2048]{1,0:T(8,128)S(1)} %get-tuple-element.12.refs_0_, f32[128,6144]{1,0:T(8,128)S(1)} %get-tuple-element.13.refs_1_, f32[256,2048]{1,0:T(8,128)S(1)} %get-tuple-element.14.refs_2_, ...), custom_call_target="tpu_custom_call" | custom-call | tf_op jit(solution)/shard_map/move_out/pallas_call | solution.py:573

commit v9 on v4

--- a/solution.py
+++ b/solution.py
@@ -23,6 +23,7 @@
 BF16 = jnp.bfloat16
 F32 = jnp.float32
 
+FAR_FIRST = (2, 5, 14, 15, 6, 1, 3, 9, 11, 8, 10, 4, 13, 12, 7, 0)
 POS, WEIGHT, BUCKET, REF, EMB, MIX = 0, 1, 2, 3, 4, 6
 KEY, QUERY, VALUE, AIM = 0, 1, 2, 3
 SLOT = {AIM: KEY, VALUE: QUERY, QUERY: VALUE, KEY: AIM}
@@ -432,12 +433,12 @@
         block = turn
         at = pl.multiple_of(block * 512, 512)
         got[SLOT[KEY], pl.ds(at, 512), :] = by_rows(at, q3.at[:, DIM : 3 * DIM]) * (1.0 / LOG2E)
-        for quarter in range(4):
-            give(KEY, block * 4 + quarter)
         pl.when(turn == 1)(exchange_sums)
         return carry
 
     lax.fori_loop(0, shards // 4, key_grad_block, 0)
+    for slot in FAR_FIRST:
+        give(KEY, slot)
 
     by_sample = jnp.concatenate(
         [

time: 106 us -> 107 us (level)
  no operation moved by 1% of the time
where the time goes in v9:
time: 107 us; the launch traced here: 106 us
  Pallas kernels  105 us (98%)
  between operations  1.45 us (1%)
    pallas_call x1, Pallas kernels, body(): pl.pallas_call(functools.partial(kernel, shards, copies), out_shape=(pltp...  102 us
    pallas_call x1, Pallas kernels, body(): pl.pallas_call(move_out, out_shape=tuple((jax.ShapeDtypeStruct(item.shape...  2.76 us

profile of v9, /device:TPU:1, one launch (start us, length us, event | category | flops | bytes accessed | tf_op | source)
XLA Modules:
  0.0 106.4 jit_solution(1336119598864400884)
XLA Ops:
  1.3 102.2 %attend.1 = (f32[128,2048]{1,0:T(8,128)S(1)}, f32[128,6144]{1,0:T(8,128)S(1)}, f32[256,2048]{1,0:T(8,128)S(1)}, f32[1,16]{1,0:T(1,128)S(1)}) custom-call(f32[128,6144]{1,0:T(8,128)} %bitcast.5, f32[128,2048]{1,0:T(8,128)} %bitcast.6, s32[1,128]{1,0:T(1,128)} %places_in.1, s32[1,128]{1,0:T(1,128)} %buckets_in.1, f32[1,128]{1,0:T(1,128)} %ref_in.1, ...), custom_call_target="tpu_custom_call" | custom-call | tf_op jit(solution)/shard_map/attend/pallas_call | solution.py:506
  103.5 2.8 %move_out.1 = (f32[128,2048]{1,0:T(8,128)}, f32[128,6144]{1,0:T(8,128)}, f32[256,2048]{1,0:T(8,128)}, f32[1,16]{1,0:T(1,128)}) custom-call(f32[128,2048]{1,0:T(8,128)S(1)} %get-tuple-element.12.refs_0_, f32[128,6144]{1,0:T(8,128)S(1)} %get-tuple-element.13.refs_1_, f32[256,2048]{1,0:T(8,128)S(1)} %get-tuple-element.14.refs_2_, ...), custom_call_target="tpu_custom_call" | custom-call | tf_op jit(solution)/shard_map/move_out/pallas_call | solution.py:558

commit v10 on v4

--- a/solution.py
+++ b/solution.py
@@ -95,11 +95,13 @@
 
     def send(part):
         pltpu.make_async_copy(source(part, me), landing(part), recv_sem.at[part]).start()
-        for peer in peers:
-            pltpu.make_async_remote_copy(
-                source(part, peer), landing(part), send_sem.at[part], recv_sem.at[part],
-                device_id={"seq": peer}, device_id_type=MESH,
-            ).start()
+        for half in range(2):
+            rows_of = pl.ds(half * (DIM // 2), DIM // 2)
+            for peer in peers:
+                pltpu.make_async_remote_copy(
+                    source(part, peer).at[rows_of], landing(part).at[rows_of], send_sem.at[part], recv_sem.at[part],
+                    device_id={"seq": peer}, device_id_type=MESH,
+                ).start()
 
     def wait_sent(part):
         sent = got.at[part, pl.ds(0, (shards - 1) * DIM), :]

time: 106 us -> 106 us (level)
  no operation moved by 1% of the time
where the time goes in v10:
time: 106 us; the launch traced here: 105 us
  Pallas kernels  104 us (98%)
  between operations  1.47 us (1%)
    pallas_call x1, Pallas kernels, body(): pl.pallas_call(functools.partial(kernel, shards, copies), out_shape=(pltp...  101 us
    pallas_call x1, Pallas kernels, body(): pl.pallas_call(move_out, out_shape=tuple((jax.ShapeDtypeStruct(item.shape...  2.76 us

profile of v10, /device:TPU:1, one launch (start us, length us, event | category | flops | bytes accessed | tf_op | source)
XLA Modules:
  0.0 105.4 jit_solution(6192018936861709110)
XLA Ops:
  1.3 101.2 %attend.1 = (f32[128,2048]{1,0:T(8,128)S(1)}, f32[128,6144]{1,0:T(8,128)S(1)}, f32[256,2048]{1,0:T(8,128)S(1)}, f32[1,16]{1,0:T(1,128)S(1)}) custom-call(f32[128,6144]{1,0:T(8,128)} %bitcast.5, f32[128,2048]{1,0:T(8,128)} %bitcast.6, s32[1,128]{1,0:T(1,128)} %places_in.1, s32[1,128]{1,0:T(1,128)} %buckets_in.1, f32[1,128]{1,0:T(1,128)} %ref_in.1, ...), custom_call_target="tpu_custom_call" | custom-call | tf_op jit(solution)/shard_map/attend/pallas_call | solution.py:507
  102.4 2.8 %move_out.1 = (f32[128,2048]{1,0:T(8,128)}, f32[128,6144]{1,0:T(8,128)}, f32[256,2048]{1,0:T(8,128)}, f32[1,16]{1,0:T(1,128)}) custom-call(f32[128,2048]{1,0:T(8,128)S(1)} %get-tuple-element.12.refs_0_, f32[128,6144]{1,0:T(8,128)S(1)} %get-tuple-element.13.refs_1_, f32[256,2048]{1,0:T(8,128)S(1)} %get-tuple-element.14.refs_2_, ...), custom_call_target="tpu_custom_call" | custom-call | tf_op jit(solution)/shard_map/move_out/pallas_call | solution.py:559

commit v11 on v9

--- a/solution.py
+++ b/solution.py
@@ -133,6 +133,8 @@
             device_id={"seq": peer}, device_id_type=MESH,
         ).start()
     send(QUERY)
+    send(VALUE)
+    send(AIM)
 
     def wait_small(sem, buffer, count, depth=2):
         taken = buffer.at[pl.ds(0, count), pl.ds(0, depth)]
@@ -219,11 +221,9 @@
         full = dot(e_hi[pl.ds(at, 512), :], right[...])
         return full[:, :DIM] + full[:, DIM:] + dot(e_lo[pl.ds(at, 512), :], right[:, 0:DIM])
 
+    reorder(KEY, 1.0, k3, kt)
     wait_sent(KEY)
-    send(VALUE)
-    reorder(KEY, 1.0, k3, kt)
     wait_sent(QUERY)
-    send(AIM)
     reorder(QUERY, SCALE * LOG2E, q3, None)
 
     def score_block(block, buffer):

time: 107 us -> 106 us (level)
  no operation moved by 1% of the time
where the time goes in v11:
time: 106 us
  Pallas kernels  105 us (99%)
  between operations  1.45 us (1%)
    pallas_call x1, Pallas kernels, body(): pl.pallas_call(functools.partial(kernel, shards, copies), out_shape=(pltp...  102 us
    pallas_call x1, Pallas kernels, body(): pl.pallas_call(move_out, out_shape=tuple((jax.ShapeDtypeStruct(item.shape...  2.76 us

profile of v11, /device:TPU:1, one launch (start us, length us, event | category | flops | bytes accessed | tf_op | source)
XLA Modules:
  0.0 106.3 jit_solution(17827899077338890293)
XLA Ops:
  1.3 102.1 %attend.1 = (f32[128,2048]{1,0:T(8,128)S(1)}, f32[128,6144]{1,0:T(8,128)S(1)}, f32[256,2048]{1,0:T(8,128)S(1)}, f32[1,16]{1,0:T(1,128)S(1)}) custom-call(f32[128,6144]{1,0:T(8,128)} %bitcast.5, f32[128,2048]{1,0:T(8,128)} %bitcast.6, s32[1,128]{1,0:T(1,128)} %places_in.1, s32[1,128]{1,0:T(1,128)} %buckets_in.1, f32[1,128]{1,0:T(1,128)} %ref_in.1, ...), custom_call_target="tpu_custom_call" | custom-call | tf_op jit(solution)/shard_map/attend/pallas_call | solution.py:506
  103.4 2.8 %move_out.1 = (f32[128,2048]{1,0:T(8,128)}, f32[128,6144]{1,0:T(8,128)}, f32[256,2048]{1,0:T(8,128)}, f32[1,16]{1,0:T(1,128)}) custom-call(f32[128,2048]{1,0:T(8,128)S(1)} %get-tuple-element.12.refs_0_, f32[128,6144]{1,0:T(8,128)S(1)} %get-tuple-element.13.refs_1_, f32[256,2048]{1,0:T(8,128)S(1)} %get-tuple-element.14.refs_2_, ...), custom_call_target="tpu_custom_call" | custom-call | tf_op jit(solution)/shard_map/move_out/pallas_call | solution.py:558
